TPU v7x, 32 devices: a whole 2x2x4 slice. The times are simulated.
32 devices in a mesh: comp: 4 (over z), dom: 8 (over y, x, core).
Axes of the slice: x: 2, y: 2, z: 4, core: 2. Of those that a mesh axis runs over, the one named last changes fastest.
Arguments:
- airside_exchange: bfloat16 [4, 4, 8192], P('comp', None, 'dom'), may hold values from -6 to 6
- regrid_matrix_partitions: bfloat16 [4, 64, 4, 128, 128], P('comp', 'dom'), may hold values from -0.25 to 0.25
- regrid_destination_latitude: int32 [4, 64, 4], P('comp', 'dom'), may hold values from 0 to 255, all different within a row
- thermal_departure: float32 [32, 256, 128], P(None, ('comp', 'dom')), may hold values from -6 to 6
- diffusivity_coefficient: float32 [31, 256, 128], P(None, ('comp', 'dom')), may hold values from 0.05 to 3
- elevation_anomaly_profile: float32 [256, 128], P(('comp', 'dom')), may hold values from -3 to 3
- depth_integrated_volume_flow: float32 [2, 256, 128], P(None, ('comp', 'dom')), may hold values from -2 to 2
- marine_indicator: int32 [256, 128], P(('comp', 'dom')), may hold values 0 or 1
Outputs:
- ocean_temperature: float32 [32, 256, 128], P(None, ('comp', 'dom'))
- ocean_height: float32 [256, 128], P(('comp', 'dom'))
- atm_surface: bfloat16 [4, 2, 8192], P('comp', None, 'dom')
Inputs may be any that keep to these rules, and one draw needn't show every extreme that they name: `regrid_destination_latitude`: each (section, source block) names 4 different ocean blocks, and every ocean block is named somewhere; ocean block b is grid row b.
All inputs are finite; a program needn't handle non-finite values. No bound on the sum of `marine_indicator` on one device may be relied on, other than what follows from the above.
Results may differ from a plain program's by a relative error of at most 0.0048.
Values may be sent and summed in bfloat16 or wider, within the bound.
A program may use at most 64 MiB of HBM per device.

v0:
```python
import jax
import jax.numpy as jnp
from jax import lax
from jax.sharding import PartitionSpec as P

NSTEP = 2
NSUB = 8


wave_gain = 0.35
stress_gain = 0.1
fresh_gain = 0.1
spread_gain = 0.2
heating_gain = 0.5


def with_halo(block, sides, width):
    for axis, dim in sides:
        count = lax.axis_size(axis)
        forward = [(i, i + 1) for i in range(count - 1)]
        backward = [(target, source) for source, target in forward]
        low = lax.ppermute(
            lax.slice_in_dim(block, block.shape[dim] - width, None, axis=dim), axis, forward
        )
        high = lax.ppermute(lax.slice_in_dim(block, 0, width, axis=dim), axis, backward)
        block = jnp.concatenate([low, block, high], axis=dim)
    return block


def vertical_solve(explicit, diffusivity_coefficient):
    levels_all = explicit.shape[0]
    solved = []
    ratios = []
    for layer_index in range(levels_all):
        upward = (
            diffusivity_coefficient[layer_index - 1]
            if layer_index > 0
            else jnp.zeros_like(explicit[0])
        )
        downward = (
            diffusivity_coefficient[layer_index]
            if layer_index < levels_all - 1
            else jnp.zeros_like(explicit[0])
        )
        pivots = 1.0 + upward + downward
        if layer_index > 0:
            pivots = pivots - upward * ratios[-1]
            solved.append((explicit[layer_index] + upward * solved[-1]) / pivots)
        else:
            solved.append(explicit[layer_index] / pivots)
        ratios.append(downward / pivots)
    result = [solved[-1]]
    for layer_index in range(levels_all - 2, -1, -1):
        result.append(solved[layer_index] + ratios[layer_index] * result[-1])
    return jnp.stack(result[::-1])


def shards(
    airside_exchange,
    regrid_matrix_partitions,
    regrid_destination_latitude,
    thermal_departure,
    diffusivity_coefficient,
    elevation_anomaly_profile,
    depth_integrated_volume_flow,
    marine_indicator,
):
    groups = lax.axis_size("comp")
    blocks_dom = lax.axis_size("dom")
    rows_here = elevation_anomaly_profile.shape[0]
    width_row = elevation_anomaly_profile.shape[1]
    fields = airside_exchange.shape[1]
    source_blocks = regrid_matrix_partitions.shape[1]
    links = regrid_matrix_partitions.shape[2]
    block_cols = regrid_matrix_partitions.shape[3]
    all_rows = groups * blocks_dom * rows_here
    sources = airside_exchange[0].reshape(fields, source_blocks, block_cols)
    weights = regrid_matrix_partitions[0]
    partial_terms = jnp.einsum(
        "fsa,skab->skfb", sources, weights, preferred_element_type=jnp.float32
    )
    partial_terms = partial_terms.reshape(source_blocks * links, fields, width_row)
    targets = regrid_destination_latitude[0].reshape(-1)
    owner_group = targets // (blocks_dom * rows_here)
    owner_block = targets // rows_here % blocks_dom
    inside_row = targets % rows_here
    placed = owner_block * (groups * rows_here) + owner_group * rows_here + inside_row
    dense_terms = (
        jnp.zeros((all_rows, fields, width_row), jnp.float32).at[placed].add(partial_terms)
    )
    block_sums = lax.psum_scatter(dense_terms, "dom", scatter_dimension=0, tiled=True)
    ocean_flux = lax.psum_scatter(block_sums, "comp", scatter_dimension=0, tiled=True)
    heating = ocean_flux[:, 0, :]
    freshwater = ocean_flux[:, 1, :]
    stress_east = ocean_flux[:, 2, :]
    stress_north = ocean_flux[:, 3, :]
    wet = marine_indicator.astype(jnp.float32)
    face_east = wet * jnp.roll(wet, -1, axis=1)
    height = elevation_anomaly_profile
    flow_east = depth_integrated_volume_flow[0]
    flow_north = depth_integrated_volume_flow[1]
    advected_quantity = thermal_departure
    face_north = None
    for outer_step in range(NSTEP):
        for substep in range(NSUB):
            extended = with_halo(
                jnp.stack([height, flow_north, wet, stress_north]), ((("comp", "dom"), 1),), 1
            )
            edge_height = extended[0]
            edge_north = extended[1]
            edge_wet = extended[2]
            edge_stress = extended[3]
            face_north = edge_wet[:-1] * edge_wet[1:]
            new_east = face_east * (
                flow_east
                - wave_gain * (jnp.roll(height, -1, axis=1) - height)
                + stress_gain * stress_east
            )
            north_rows = face_north * (
                edge_north[:-1]
                - wave_gain * (edge_height[1:] - edge_height[:-1])
                + stress_gain * edge_stress[:-1]
            )
            height = (
                height
                - wave_gain
                * (new_east - jnp.roll(new_east, 1, axis=1) + north_rows[1:] - north_rows[:-1])
                + fresh_gain * freshwater * wet
            )
            flow_east = new_east
            flow_north = north_rows[1:]
        edge_tracer = with_halo(advected_quantity, ((("comp", "dom"), 1),), 1)
        along_east = face_east * (jnp.roll(advected_quantity, -1, axis=2) - advected_quantity)
        along_north = face_north * (edge_tracer[:, 1:] - edge_tracer[:, :-1])
        laplace = (
            along_east - jnp.roll(along_east, 1, axis=2) + along_north[:, 1:] - along_north[:, :-1]
        )
        explicit = advected_quantity + spread_gain * laplace
        explicit = explicit.at[0].add(heating_gain * heating * wet)
        advected_quantity = vertical_solve(explicit, diffusivity_coefficient)
    surface = jnp.stack([advected_quantity[0], height]).astype(jnp.bfloat16)
    shard_rows = lax.all_gather(surface, ("comp", "dom"), axis=1, tiled=True)
    count_rows = shard_rows.shape[1]
    selector = (targets[:, None] == jnp.arange(count_rows, dtype=jnp.int32)[None, :]).astype(
        jnp.bfloat16
    )
    picked = jnp.einsum("nr,frb->nfb", selector, shard_rows, preferred_element_type=jnp.float32)
    chosen = picked.astype(jnp.bfloat16).reshape(source_blocks, links, 2, width_row)
    returned = jnp.einsum("skfb,skab->fsa", chosen, weights, preferred_element_type=jnp.float32)
    return (
        advected_quantity,
        height,
        returned.reshape(1, 2, source_blocks * block_cols).astype(jnp.bfloat16),
    )


def solution(mesh):
    return jax.shard_map(
        shards,
        mesh=mesh,
        in_specs=(
            P("comp", None, "dom"),
            P("comp", "dom", None, None, None),
            P("comp", "dom", None),
            P(None, ("comp", "dom"), None),
            P(None, ("comp", "dom"), None),
            P(("comp", "dom"), None),
            P(None, ("comp", "dom"), None),
            P(("comp", "dom"), None),
        ),
        out_specs=(
            P(None, ("comp", "dom"), None),
            P(("comp", "dom"), None),
            P("comp", None, "dom"),
        ),
        check_vma=False,
    )
```

profile of v0, /device:TPU:0, one launch (start us, length us, event | category | flops | bytes accessed | tf_op | source)
XLA Modules:
  0.0 258.4 jit_solution(18159484786546370690)
XLA Ops:
  7.2 0.8 copy.16
  8.7 1.6 scatter_fusion
  10.4 0.8 copy.18
  11.3 0.8 copy-done.1
  12.2 1.3 collective-permute-start.16
  13.5 3.0 %collective-permute-start.17 = (f32[32,1,128]{2,1,0:T(1,128)S(1)}, f32[32,1,128]{2,1,0:T(1,128)S(1)}, u32[]{:S(2)}, u32[]{:S(2)}) collective-permute-start(f32[32,1,128]{2,1,0:T(1,128)S(1)} %get-tuple-element.178), channel_id=1, source_target_pairs={{0,1},{1,2},{2,3},{3,4},{4,5},{5,6},{6,7},{7,8},{8,9},{9,10},{10,1... | collective-permute-start | bytes 49160 | tf_op jit(solution)/shard_map/ppermute | solution.py:22
  16.7 31.5 %reduce-scatter.3.cloned.1.call-done = f32[32,4,128]{2,0,1:T(8,128)} async-done(((f32[256,4,128]{2,0,1:T(8,128)}), f32[32,4,128]{2,0,1:T(8,128)}) %reduce-scatter.3.cloned.1.call-update) | async-done | bytes 65552 | tf_op jit(solution)/shard_map/reduce_scatter | solution.py:91
  48.3 0.7 copy-done.5
  49.7 20.0 %reduce-scatter.5.cloned.1.call-done = f32[8,4,128]{2,0,1:T(8,128)} async-done(((f32[32,4,128]{2,0,1:T(8,128)}), f32[8,4,128]{2,0,1:T(8,128)}) %reduce-scatter.5.cloned.1.call-update) | async-done | bytes 16400 | tf_op jit(solution)/shard_map/reduce_scatter | solution.py:92
  69.7 0.7 slice_bitcast_fusion.14
  70.3 1.3 collective-permute-start
  71.6 1.3 collective-permute-start.1
  73.3 3.1 %collective-permute-done.1 = f32[4,1,128]{2,1,0:T(1,128)S(1)} collective-permute-done((f32[4,1,128]{2,1,0:T(1,128)S(1)}, f32[4,1,128]{2,1,0:T(1,128)S(1)}, u32[]{:S(2)}, u32[]{:S(2)}) %collective-permute-start.1) | collective-permute-done | bytes 2080 | tf_op jit(solution)/shard_map/ppermute | solution.py:25
  76.6 4.3 %collective-permute-start.2 = (f32[4,1,128]{2,1,0:T(1,128)S(1)}, f32[4,1,128]{2,1,0:T(1,128)S(1)}, u32[]{:S(2)}, u32[]{:S(2)}) collective-permute-start(f32[4,1,128]{2,1,0:T(1,128)S(1)} %get-tuple-element.239), channel_id=1, source_target_pairs={{0,1},{1,2},{2,3},{3,4},{4,5},{5,6},{6,7},{7,8},{8,9},{9,10},{10,1... | collective-permute-start | bytes 6152 | tf_op jit(solution)/shard_map/ppermute | solution.py:22
  80.9 1.3 collective-permute-start.3
  82.4 1.6 collective-permute-done.3
  84.2 4.5 %collective-permute-start.4 = (f32[4,1,128]{2,1,0:T(1,128)S(1)}, f32[4,1,128]{2,1,0:T(1,128)S(1)}, u32[]{:S(2)}, u32[]{:S(2)}) collective-permute-start(f32[4,1,128]{2,1,0:T(1,128)S(1)} %get-tuple-element.235), channel_id=1, source_target_pairs={{0,1},{1,2},{2,3},{3,4},{4,5},{5,6},{6,7},{7,8},{8,9},{9,10},{10,1... | collective-permute-start | bytes 6152 | tf_op jit(solution)/shard_map/ppermute | solution.py:22
  88.6 1.3 collective-permute-start.5
  90.1 1.6 collective-permute-done.5
  91.9 4.7 %collective-permute-start.6 = (f32[4,1,128]{2,1,0:T(1,128)S(1)}, f32[4,1,128]{2,1,0:T(1,128)S(1)}, u32[]{:S(2)}, u32[]{:S(2)}) collective-permute-start(f32[4,1,128]{2,1,0:T(1,128)S(1)} %get-tuple-element.231), channel_id=1, source_target_pairs={{0,1},{1,2},{2,3},{3,4},{4,5},{5,6},{6,7},{7,8},{8,9},{9,10},{10,1... | collective-permute-start | bytes 6152 | tf_op jit(solution)/shard_map/ppermute | solution.py:22
  96.6 1.3 collective-permute-start.7
  98.1 1.6 collective-permute-done.7
  99.9 4.7 %collective-permute-start.8 = (f32[4,1,128]{2,1,0:T(1,128)S(1)}, f32[4,1,128]{2,1,0:T(1,128)S(1)}, u32[]{:S(2)}, u32[]{:S(2)}) collective-permute-start(f32[4,1,128]{2,1,0:T(1,128)S(1)} %get-tuple-element.227), channel_id=1, source_target_pairs={{0,1},{1,2},{2,3},{3,4},{4,5},{5,6},{6,7},{7,8},{8,9},{9,10},{10,1... | collective-permute-start | bytes 6152 | tf_op jit(solution)/shard_map/ppermute | solution.py:22
  104.6 1.3 collective-permute-start.9
  106.1 1.6 collective-permute-done.9
  107.9 4.7 %collective-permute-start.10 = (f32[4,1,128]{2,1,0:T(1,128)S(1)}, f32[4,1,128]{2,1,0:T(1,128)S(1)}, u32[]{:S(2)}, u32[]{:S(2)}) collective-permute-start(f32[4,1,128]{2,1,0:T(1,128)S(1)} %get-tuple-element.223), channel_id=1, source_target_pairs={{0,1},{1,2},{2,3},{3,4},{4,5},{5,6},{6,7},{7,8},{8,9},{9,10},{10,1... | collective-permute-start | bytes 6152 | tf_op jit(solution)/shard_map/ppermute | solution.py:22
  112.6 1.3 collective-permute-start.11
  114.0 1.6 collective-permute-done.11
  115.8 4.7 %collective-permute-start.12 = (f32[4,1,128]{2,1,0:T(1,128)S(1)}, f32[4,1,128]{2,1,0:T(1,128)S(1)}, u32[]{:S(2)}, u32[]{:S(2)}) collective-permute-start(f32[4,1,128]{2,1,0:T(1,128)S(1)} %get-tuple-element.219), channel_id=1, source_target_pairs={{0,1},{1,2},{2,3},{3,4},{4,5},{5,6},{6,7},{7,8},{8,9},{9,10},{10,1... | collective-permute-start | bytes 6152 | tf_op jit(solution)/shard_map/ppermute | solution.py:22
  120.5 1.3 collective-permute-start.13
  122.0 1.6 collective-permute-done.13
  123.8 4.7 %collective-permute-start.14 = (f32[4,1,128]{2,1,0:T(1,128)S(1)}, f32[4,1,128]{2,1,0:T(1,128)S(1)}, u32[]{:S(2)}, u32[]{:S(2)}) collective-permute-start(f32[4,1,128]{2,1,0:T(1,128)S(1)} %get-tuple-element.215), channel_id=1, source_target_pairs={{0,1},{1,2},{2,3},{3,4},{4,5},{5,6},{6,7},{7,8},{8,9},{9,10},{10,1... | collective-permute-start | bytes 6152 | tf_op jit(solution)/shard_map/ppermute | solution.py:22
  128.5 1.3 collective-permute-start.15
  130.0 1.6 collective-permute-done.15
  131.8 0.8 copy-done.2
  133.6 4.7 %collective-permute-start.18 = (f32[4,1,128]{2,1,0:T(1,128)S(1)}, f32[4,1,128]{2,1,0:T(1,128)S(1)}, u32[]{:S(2)}, u32[]{:S(2)}) collective-permute-start(f32[4,1,128]{2,1,0:T(1,128)S(1)} %get-tuple-element.211), channel_id=1, source_target_pairs={{0,1},{1,2},{2,3},{3,4},{4,5},{5,6},{6,7},{7,8},{8,9},{9,10},{10,1... | collective-permute-start | bytes 6152 | tf_op jit(solution)/shard_map/ppermute | solution.py:22
  138.4 1.3 collective-permute-start.19
  140.0 1.3 collective-permute-start.34
  141.3 3.7 %collective-permute-start.35 = (f32[32,1,128]{2,1,0:T(1,128)S(1)}, f32[32,1,128]{2,1,0:T(1,128)S(1)}, u32[]{:S(2)}, u32[]{:S(2)}) collective-permute-start(f32[32,1,128]{2,1,0:T(1,128)S(1)} %get-tuple-element.176), channel_id=1, source_target_pairs={{0,1},{1,2},{2,3},{3,4},{4,5},{5,6},{6,7},{7,8},{8,9},{9,10},{10,1... | collective-permute-start | bytes 49160 | tf_op jit(solution)/shard_map/ppermute | solution.py:22
  145.2 4.5 %collective-permute-start.20 = (f32[4,1,128]{2,1,0:T(1,128)S(1)}, f32[4,1,128]{2,1,0:T(1,128)S(1)}, u32[]{:S(2)}, u32[]{:S(2)}) collective-permute-start(f32[4,1,128]{2,1,0:T(1,128)S(1)} %get-tuple-element.207), channel_id=1, source_target_pairs={{0,1},{1,2},{2,3},{3,4},{4,5},{5,6},{6,7},{7,8},{8,9},{9,10},{10,1... | collective-permute-start | bytes 6152 | tf_op jit(solution)/shard_map/ppermute | solution.py:22
  149.7 1.3 collective-permute-start.21
  151.2 1.6 collective-permute-done.21
  153.0 5.6 %collective-permute-start.22 = (f32[4,1,128]{2,1,0:T(1,128)S(1)}, f32[4,1,128]{2,1,0:T(1,128)S(1)}, u32[]{:S(2)}, u32[]{:S(2)}) collective-permute-start(f32[4,1,128]{2,1,0:T(1,128)S(1)} %get-tuple-element.203), channel_id=1, source_target_pairs={{0,1},{1,2},{2,3},{3,4},{4,5},{5,6},{6,7},{7,8},{8,9},{9,10},{10,1... | collective-permute-start | bytes 6152 | tf_op jit(solution)/shard_map/ppermute | solution.py:22
  158.6 1.3 collective-permute-start.23
  160.1 1.6 collective-permute-done.23
  161.9 5.6 %collective-permute-start.24 = (f32[4,1,128]{2,1,0:T(1,128)S(1)}, f32[4,1,128]{2,1,0:T(1,128)S(1)}, u32[]{:S(2)}, u32[]{:S(2)}) collective-permute-start(f32[4,1,128]{2,1,0:T(1,128)S(1)} %get-tuple-element.199), channel_id=1, source_target_pairs={{0,1},{1,2},{2,3},{3,4},{4,5},{5,6},{6,7},{7,8},{8,9},{9,10},{10,1... | collective-permute-start | bytes 6152 | tf_op jit(solution)/shard_map/ppermute | solution.py:22
  167.5 1.3 collective-permute-start.25
  169.0 1.6 collective-permute-done.25
  170.8 6.1 %collective-permute-start.26 = (f32[4,1,128]{2,1,0:T(1,128)S(1)}, f32[4,1,128]{2,1,0:T(1,128)S(1)}, u32[]{:S(2)}, u32[]{:S(2)}) collective-permute-start(f32[4,1,128]{2,1,0:T(1,128)S(1)} %get-tuple-element.195), channel_id=1, source_target_pairs={{0,1},{1,2},{2,3},{3,4},{4,5},{5,6},{6,7},{7,8},{8,9},{9,10},{10,1... | collective-permute-start | bytes 6152 | tf_op jit(solution)/shard_map/ppermute | solution.py:22
  176.8 1.3 collective-permute-start.27
  178.3 1.6 collective-permute-done.27
  180.1 5.6 %collective-permute-start.28 = (f32[4,1,128]{2,1,0:T(1,128)S(1)}, f32[4,1,128]{2,1,0:T(1,128)S(1)}, u32[]{:S(2)}, u32[]{:S(2)}) collective-permute-start(f32[4,1,128]{2,1,0:T(1,128)S(1)} %get-tuple-element.191), channel_id=1, source_target_pairs={{0,1},{1,2},{2,3},{3,4},{4,5},{5,6},{6,7},{7,8},{8,9},{9,10},{10,1... | collective-permute-start | bytes 6152 | tf_op jit(solution)/shard_map/ppermute | solution.py:22
  185.7 1.3 collective-permute-start.29
  187.2 1.6 collective-permute-done.29
  189.0 5.6 %collective-permute-start.30 = (f32[4,1,128]{2,1,0:T(1,128)S(1)}, f32[4,1,128]{2,1,0:T(1,128)S(1)}, u32[]{:S(2)}, u32[]{:S(2)}) collective-permute-start(f32[4,1,128]{2,1,0:T(1,128)S(1)} %get-tuple-element.187), channel_id=1, source_target_pairs={{0,1},{1,2},{2,3},{3,4},{4,5},{5,6},{6,7},{7,8},{8,9},{9,10},{10,1... | collective-permute-start | bytes 6152 | tf_op jit(solution)/shard_map/ppermute | solution.py:22
  194.6 1.3 collective-permute-start.31
  196.0 1.6 collective-permute-done.31
  197.8 5.6 %collective-permute-start.32 = (f32[4,1,128]{2,1,0:T(1,128)S(1)}, f32[4,1,128]{2,1,0:T(1,128)S(1)}, u32[]{:S(2)}, u32[]{:S(2)}) collective-permute-start(f32[4,1,128]{2,1,0:T(1,128)S(1)} %get-tuple-element.183), channel_id=1, source_target_pairs={{0,1},{1,2},{2,3},{3,4},{4,5},{5,6},{6,7},{7,8},{8,9},{9,10},{10,1... | collective-permute-start | bytes 6152 | tf_op jit(solution)/shard_map/ppermute | solution.py:22
  203.4 1.3 collective-permute-start.33
  204.9 1.6 collective-permute-done.33
  206.5 0.7 convert_bitcast_fusion
  207.7 41.7 %all_gather.3 = bf16[2,256,128]{2,1,0:T(8,128)(2,1)S(1)} all-gather(bf16[2,8,128]{2,1,0:T(8,128)(2,1)S(1)} %pad_maximum_fusion.96), channel_id=1, replica_groups=mesh['comp'=4,'dom'=8] {'comp','dom'}, dimensions={1}, use_global_device_ids=true | all-gather | bytes 135168 | tf_op jit(solution)/shard_map/all_gather | solution.py:142
  249.6 1.0 fusion.1
  251.0 0.6 copy-done.8
  (269 shorter events, 9.2 us)
Async XLA Ops:
  7.2 1.2 copy-start
  7.2 1.2 copy-start.6
  7.2 41.0 %reduce-scatter.3.cloned.1.call-start = ((), (), s32[]{:S(2)}) async-start(), calls=%async_computation.2 | async-start | bytes 589824 | tf_op jit(solution)/shard_map/reduce_scatter | solution.py:91
  11.2 0.9 copy-start.1
  11.2 58.4 %reduce-scatter.5.cloned.1.call-start = ((), (), s32[]{:S(2)}) async-start(), calls=%async_computation.3 | async-start | bytes 81920 | tf_op jit(solution)/shard_map/reduce_scatter | solution.py:92
  12.2 119.4 %collective-permute-start.16 = (f32[32,1,128]{2,1,0:T(1,128)S(1)}, f32[32,1,128]{2,1,0:T(1,128)S(1)}, u32[]{:S(2)}, u32[]{:S(2)}) collective-permute-start(f32[32,1,128]{2,1,0:T(1,128)S(1)} %get-tuple-element.179), channel_id=1, source_target_pairs={{1,0},{2,1},{3,2},{4,3},{5,4},{6,5},{7,6},{8,7},{9,8},{10,9},{11,1... | collective-permute-start | bytes 49160 | tf_op jit(solution)/shard_map/ppermute | solution.py:25
  13.4 3.2 %copy-start.7 = (f32[2,8,128]{2,1,0:T(8,128)S(1)}, f32[2,8,128]{2,1,0:T(8,128)}, u32[]{:S(2)}) copy-start(f32[2,8,128]{2,1,0:T(8,128)} %param.18) | copy-start | bytes 24580
  13.5 118.1 %collective-permute-start.17 = (f32[32,1,128]{2,1,0:T(1,128)S(1)}, f32[32,1,128]{2,1,0:T(1,128)S(1)}, u32[]{:S(2)}, u32[]{:S(2)}) collective-permute-start(f32[32,1,128]{2,1,0:T(1,128)S(1)} %get-tuple-element.178), channel_id=1, source_target_pairs={{0,1},{1,2},{2,3},{3,4},{4,5},{5,6},{6,7},{7,8},{8,9},{9,10},{10,1... | collective-permute-start | bytes 49160 | tf_op jit(solution)/shard_map/ppermute | solution.py:22
  48.2 0.7 copy-start.5
  48.9 0.7 copy-start.4
  70.3 2.6 %copy-start.3 = (f32[8,4,128]{2,0,1:T(8,128)S(1)}, f32[8,4,128]{2,0,1:T(8,128)}, u32[]{:S(2)}) copy-start(f32[8,4,128]{2,0,1:T(8,128)} %reduce-scatter.5.cloned.1.call-done) | copy-start | bytes 49156
  70.3 3.0 %collective-permute-start = (f32[4,1,128]{2,1,0:T(1,128)S(1)}, f32[4,1,128]{2,1,0:T(1,128)S(1)}, u32[]{:S(2)}, u32[]{:S(2)}) collective-permute-start(f32[4,1,128]{2,1,0:T(1,128)S(1)} %get-tuple-element.243), channel_id=1, source_target_pairs={{0,1},{1,2},{2,3},{3,4},{4,5},{5,6},{6,7},{7,8},{8,9},{9,10},{10,1... | collective-permute-start | bytes 6152 | tf_op jit(solution)/shard_map/ppermute | solution.py:22
  71.6 4.8 %collective-permute-start.1 = (f32[4,1,128]{2,1,0:T(1,128)S(1)}, f32[4,1,128]{2,1,0:T(1,128)S(1)}, u32[]{:S(2)}, u32[]{:S(2)}) collective-permute-start(f32[4,1,128]{2,1,0:T(1,128)S(1)} %get-tuple-element.242), channel_id=1, source_target_pairs={{1,0},{2,1},{3,2},{4,3},{5,4},{6,5},{7,6},{8,7},{9,8},{10,9},{11,1... | collective-permute-start | bytes 6152 | tf_op jit(solution)/shard_map/ppermute | solution.py:25
  76.6 5.7 %collective-permute-start.2 = (f32[4,1,128]{2,1,0:T(1,128)S(1)}, f32[4,1,128]{2,1,0:T(1,128)S(1)}, u32[]{:S(2)}, u32[]{:S(2)}) collective-permute-start(f32[4,1,128]{2,1,0:T(1,128)S(1)} %get-tuple-element.239), channel_id=1, source_target_pairs={{0,1},{1,2},{2,3},{3,4},{4,5},{5,6},{6,7},{7,8},{8,9},{9,10},{10,1... | collective-permute-start | bytes 6152 | tf_op jit(solution)/shard_map/ppermute | solution.py:22
  80.9 3.1 %collective-permute-start.3 = (f32[4,1,128]{2,1,0:T(1,128)S(1)}, f32[4,1,128]{2,1,0:T(1,128)S(1)}, u32[]{:S(2)}, u32[]{:S(2)}) collective-permute-start(f32[4,1,128]{2,1,0:T(1,128)S(1)} %get-tuple-element.238), channel_id=1, source_target_pairs={{1,0},{2,1},{3,2},{4,3},{5,4},{6,5},{7,6},{8,7},{9,8},{10,9},{11,1... | collective-permute-start | bytes 6152 | tf_op jit(solution)/shard_map/ppermute | solution.py:25
  84.2 5.9 %collective-permute-start.4 = (f32[4,1,128]{2,1,0:T(1,128)S(1)}, f32[4,1,128]{2,1,0:T(1,128)S(1)}, u32[]{:S(2)}, u32[]{:S(2)}) collective-permute-start(f32[4,1,128]{2,1,0:T(1,128)S(1)} %get-tuple-element.235), channel_id=1, source_target_pairs={{0,1},{1,2},{2,3},{3,4},{4,5},{5,6},{6,7},{7,8},{8,9},{9,10},{10,1... | collective-permute-start | bytes 6152 | tf_op jit(solution)/shard_map/ppermute | solution.py:22
  88.6 3.1 %collective-permute-start.5 = (f32[4,1,128]{2,1,0:T(1,128)S(1)}, f32[4,1,128]{2,1,0:T(1,128)S(1)}, u32[]{:S(2)}, u32[]{:S(2)}) collective-permute-start(f32[4,1,128]{2,1,0:T(1,128)S(1)} %get-tuple-element.234), channel_id=1, source_target_pairs={{1,0},{2,1},{3,2},{4,3},{5,4},{6,5},{7,6},{8,7},{9,8},{10,9},{11,1... | collective-permute-start | bytes 6152 | tf_op jit(solution)/shard_map/ppermute | solution.py:25
  91.9 6.2 %collective-permute-start.6 = (f32[4,1,128]{2,1,0:T(1,128)S(1)}, f32[4,1,128]{2,1,0:T(1,128)S(1)}, u32[]{:S(2)}, u32[]{:S(2)}) collective-permute-start(f32[4,1,128]{2,1,0:T(1,128)S(1)} %get-tuple-element.231), channel_id=1, source_target_pairs={{0,1},{1,2},{2,3},{3,4},{4,5},{5,6},{6,7},{7,8},{8,9},{9,10},{10,1... | collective-permute-start | bytes 6152 | tf_op jit(solution)/shard_map/ppermute | solution.py:22
  96.6 3.1 %collective-permute-start.7 = (f32[4,1,128]{2,1,0:T(1,128)S(1)}, f32[4,1,128]{2,1,0:T(1,128)S(1)}, u32[]{:S(2)}, u32[]{:S(2)}) collective-permute-start(f32[4,1,128]{2,1,0:T(1,128)S(1)} %get-tuple-element.230), channel_id=1, source_target_pairs={{1,0},{2,1},{3,2},{4,3},{5,4},{6,5},{7,6},{8,7},{9,8},{10,9},{11,1... | collective-permute-start | bytes 6152 | tf_op jit(solution)/shard_map/ppermute | solution.py:25
  99.9 6.2 %collective-permute-start.8 = (f32[4,1,128]{2,1,0:T(1,128)S(1)}, f32[4,1,128]{2,1,0:T(1,128)S(1)}, u32[]{:S(2)}, u32[]{:S(2)}) collective-permute-start(f32[4,1,128]{2,1,0:T(1,128)S(1)} %get-tuple-element.227), channel_id=1, source_target_pairs={{0,1},{1,2},{2,3},{3,4},{4,5},{5,6},{6,7},{7,8},{8,9},{9,10},{10,1... | collective-permute-start | bytes 6152 | tf_op jit(solution)/shard_map/ppermute | solution.py:22
  104.6 3.1 %collective-permute-start.9 = (f32[4,1,128]{2,1,0:T(1,128)S(1)}, f32[4,1,128]{2,1,0:T(1,128)S(1)}, u32[]{:S(2)}, u32[]{:S(2)}) collective-permute-start(f32[4,1,128]{2,1,0:T(1,128)S(1)} %get-tuple-element.226), channel_id=1, source_target_pairs={{1,0},{2,1},{3,2},{4,3},{5,4},{6,5},{7,6},{8,7},{9,8},{10,9},{11,1... | collective-permute-start | bytes 6152 | tf_op jit(solution)/shard_map/ppermute | solution.py:25
  107.9 6.2 %collective-permute-start.10 = (f32[4,1,128]{2,1,0:T(1,128)S(1)}, f32[4,1,128]{2,1,0:T(1,128)S(1)}, u32[]{:S(2)}, u32[]{:S(2)}) collective-permute-start(f32[4,1,128]{2,1,0:T(1,128)S(1)} %get-tuple-element.223), channel_id=1, source_target_pairs={{0,1},{1,2},{2,3},{3,4},{4,5},{5,6},{6,7},{7,8},{8,9},{9,10},{10,1... | collective-permute-start | bytes 6152 | tf_op jit(solution)/shard_map/ppermute | solution.py:22
  112.6 3.1 %collective-permute-start.11 = (f32[4,1,128]{2,1,0:T(1,128)S(1)}, f32[4,1,128]{2,1,0:T(1,128)S(1)}, u32[]{:S(2)}, u32[]{:S(2)}) collective-permute-start(f32[4,1,128]{2,1,0:T(1,128)S(1)} %get-tuple-element.222), channel_id=1, source_target_pairs={{1,0},{2,1},{3,2},{4,3},{5,4},{6,5},{7,6},{8,7},{9,8},{10,9},{11,1... | collective-permute-start | bytes 6152 | tf_op jit(solution)/shard_map/ppermute | solution.py:25
  115.8 6.2 %collective-permute-start.12 = (f32[4,1,128]{2,1,0:T(1,128)S(1)}, f32[4,1,128]{2,1,0:T(1,128)S(1)}, u32[]{:S(2)}, u32[]{:S(2)}) collective-permute-start(f32[4,1,128]{2,1,0:T(1,128)S(1)} %get-tuple-element.219), channel_id=1, source_target_pairs={{0,1},{1,2},{2,3},{3,4},{4,5},{5,6},{6,7},{7,8},{8,9},{9,10},{10,1... | collective-permute-start | bytes 6152 | tf_op jit(solution)/shard_map/ppermute | solution.py:22
  120.5 3.1 %collective-permute-start.13 = (f32[4,1,128]{2,1,0:T(1,128)S(1)}, f32[4,1,128]{2,1,0:T(1,128)S(1)}, u32[]{:S(2)}, u32[]{:S(2)}) collective-permute-start(f32[4,1,128]{2,1,0:T(1,128)S(1)} %get-tuple-element.218), channel_id=1, source_target_pairs={{1,0},{2,1},{3,2},{4,3},{5,4},{6,5},{7,6},{8,7},{9,8},{10,9},{11,1... | collective-permute-start | bytes 6152 | tf_op jit(solution)/shard_map/ppermute | solution.py:25
  123.8 6.2 %collective-permute-start.14 = (f32[4,1,128]{2,1,0:T(1,128)S(1)}, f32[4,1,128]{2,1,0:T(1,128)S(1)}, u32[]{:S(2)}, u32[]{:S(2)}) collective-permute-start(f32[4,1,128]{2,1,0:T(1,128)S(1)} %get-tuple-element.215), channel_id=1, source_target_pairs={{0,1},{1,2},{2,3},{3,4},{4,5},{5,6},{6,7},{7,8},{8,9},{9,10},{10,1... | collective-permute-start | bytes 6152 | tf_op jit(solution)/shard_map/ppermute | solution.py:22
  128.5 3.1 %collective-permute-start.15 = (f32[4,1,128]{2,1,0:T(1,128)S(1)}, f32[4,1,128]{2,1,0:T(1,128)S(1)}, u32[]{:S(2)}, u32[]{:S(2)}) collective-permute-start(f32[4,1,128]{2,1,0:T(1,128)S(1)} %get-tuple-element.214), channel_id=1, source_target_pairs={{1,0},{2,1},{3,2},{4,3},{5,4},{6,5},{7,6},{8,7},{9,8},{10,9},{11,1... | collective-permute-start | bytes 6152 | tf_op jit(solution)/shard_map/ppermute | solution.py:25
  131.7 0.9 copy-start.2
  133.6 11.3 %collective-permute-start.18 = (f32[4,1,128]{2,1,0:T(1,128)S(1)}, f32[4,1,128]{2,1,0:T(1,128)S(1)}, u32[]{:S(2)}, u32[]{:S(2)}) collective-permute-start(f32[4,1,128]{2,1,0:T(1,128)S(1)} %get-tuple-element.211), channel_id=1, source_target_pairs={{0,1},{1,2},{2,3},{3,4},{4,5},{5,6},{6,7},{7,8},{8,9},{9,10},{10,1... | collective-permute-start | bytes 6152 | tf_op jit(solution)/shard_map/ppermute | solution.py:22
  138.4 6.6 %collective-permute-start.19 = (f32[4,1,128]{2,1,0:T(1,128)S(1)}, f32[4,1,128]{2,1,0:T(1,128)S(1)}, u32[]{:S(2)}, u32[]{:S(2)}) collective-permute-start(f32[4,1,128]{2,1,0:T(1,128)S(1)} %get-tuple-element.210), channel_id=1, source_target_pairs={{1,0},{2,1},{3,2},{4,3},{5,4},{6,5},{7,6},{8,7},{9,8},{10,9},{11,1... | collective-permute-start | bytes 6152 | tf_op jit(solution)/shard_map/ppermute | solution.py:25
  140.0 67.2 %collective-permute-start.34 = (f32[32,1,128]{2,1,0:T(1,128)S(1)}, f32[32,1,128]{2,1,0:T(1,128)S(1)}, u32[]{:S(2)}, u32[]{:S(2)}) collective-permute-start(f32[32,1,128]{2,1,0:T(1,128)S(1)} %get-tuple-element.177), channel_id=1, source_target_pairs={{1,0},{2,1},{3,2},{4,3},{5,4},{6,5},{7,6},{8,7},{9,8},{10,9},{11,1... | collective-permute-start | bytes 49160 | tf_op jit(solution)/shard_map/ppermute | solution.py:25
  141.3 65.9 %collective-permute-start.35 = (f32[32,1,128]{2,1,0:T(1,128)S(1)}, f32[32,1,128]{2,1,0:T(1,128)S(1)}, u32[]{:S(2)}, u32[]{:S(2)}) collective-permute-start(f32[32,1,128]{2,1,0:T(1,128)S(1)} %get-tuple-element.176), channel_id=1, source_target_pairs={{0,1},{1,2},{2,3},{3,4},{4,5},{5,6},{6,7},{7,8},{8,9},{9,10},{10,1... | collective-permute-start | bytes 49160 | tf_op jit(solution)/shard_map/ppermute | solution.py:22
  145.2 6.0 %collective-permute-start.20 = (f32[4,1,128]{2,1,0:T(1,128)S(1)}, f32[4,1,128]{2,1,0:T(1,128)S(1)}, u32[]{:S(2)}, u32[]{:S(2)}) collective-permute-start(f32[4,1,128]{2,1,0:T(1,128)S(1)} %get-tuple-element.207), channel_id=1, source_target_pairs={{0,1},{1,2},{2,3},{3,4},{4,5},{5,6},{6,7},{7,8},{8,9},{9,10},{10,1... | collective-permute-start | bytes 6152 | tf_op jit(solution)/shard_map/ppermute | solution.py:22
  149.7 3.1 %collective-permute-start.21 = (f32[4,1,128]{2,1,0:T(1,128)S(1)}, f32[4,1,128]{2,1,0:T(1,128)S(1)}, u32[]{:S(2)}, u32[]{:S(2)}) collective-permute-start(f32[4,1,128]{2,1,0:T(1,128)S(1)} %get-tuple-element.206), channel_id=1, source_target_pairs={{1,0},{2,1},{3,2},{4,3},{5,4},{6,5},{7,6},{8,7},{9,8},{10,9},{11,1... | collective-permute-start | bytes 6152 | tf_op jit(solution)/shard_map/ppermute | solution.py:25
  153.0 7.1 %collective-permute-start.22 = (f32[4,1,128]{2,1,0:T(1,128)S(1)}, f32[4,1,128]{2,1,0:T(1,128)S(1)}, u32[]{:S(2)}, u32[]{:S(2)}) collective-permute-start(f32[4,1,128]{2,1,0:T(1,128)S(1)} %get-tuple-element.203), channel_id=1, source_target_pairs={{0,1},{1,2},{2,3},{3,4},{4,5},{5,6},{6,7},{7,8},{8,9},{9,10},{10,1... | collective-permute-start | bytes 6152 | tf_op jit(solution)/shard_map/ppermute | solution.py:22
  158.6 3.1 %collective-permute-start.23 = (f32[4,1,128]{2,1,0:T(1,128)S(1)}, f32[4,1,128]{2,1,0:T(1,128)S(1)}, u32[]{:S(2)}, u32[]{:S(2)}) collective-permute-start(f32[4,1,128]{2,1,0:T(1,128)S(1)} %get-tuple-element.202), channel_id=1, source_target_pairs={{1,0},{2,1},{3,2},{4,3},{5,4},{6,5},{7,6},{8,7},{9,8},{10,9},{11,1... | collective-permute-start | bytes 6152 | tf_op jit(solution)/shard_map/ppermute | solution.py:25
  161.9 7.1 %collective-permute-start.24 = (f32[4,1,128]{2,1,0:T(1,128)S(1)}, f32[4,1,128]{2,1,0:T(1,128)S(1)}, u32[]{:S(2)}, u32[]{:S(2)}) collective-permute-start(f32[4,1,128]{2,1,0:T(1,128)S(1)} %get-tuple-element.199), channel_id=1, source_target_pairs={{0,1},{1,2},{2,3},{3,4},{4,5},{5,6},{6,7},{7,8},{8,9},{9,10},{10,1... | collective-permute-start | bytes 6152 | tf_op jit(solution)/shard_map/ppermute | solution.py:22
  167.5 3.1 %collective-permute-start.25 = (f32[4,1,128]{2,1,0:T(1,128)S(1)}, f32[4,1,128]{2,1,0:T(1,128)S(1)}, u32[]{:S(2)}, u32[]{:S(2)}) collective-permute-start(f32[4,1,128]{2,1,0:T(1,128)S(1)} %get-tuple-element.198), channel_id=1, source_target_pairs={{1,0},{2,1},{3,2},{4,3},{5,4},{6,5},{7,6},{8,7},{9,8},{10,9},{11,1... | collective-permute-start | bytes 6152 | tf_op jit(solution)/shard_map/ppermute | solution.py:25
  170.8 7.5 %collective-permute-start.26 = (f32[4,1,128]{2,1,0:T(1,128)S(1)}, f32[4,1,128]{2,1,0:T(1,128)S(1)}, u32[]{:S(2)}, u32[]{:S(2)}) collective-permute-start(f32[4,1,128]{2,1,0:T(1,128)S(1)} %get-tuple-element.195), channel_id=1, source_target_pairs={{0,1},{1,2},{2,3},{3,4},{4,5},{5,6},{6,7},{7,8},{8,9},{9,10},{10,1... | collective-permute-start | bytes 6152 | tf_op jit(solution)/shard_map/ppermute | solution.py:22
  176.8 3.1 %collective-permute-start.27 = (f32[4,1,128]{2,1,0:T(1,128)S(1)}, f32[4,1,128]{2,1,0:T(1,128)S(1)}, u32[]{:S(2)}, u32[]{:S(2)}) collective-permute-start(f32[4,1,128]{2,1,0:T(1,128)S(1)} %get-tuple-element.194), channel_id=1, source_target_pairs={{1,0},{2,1},{3,2},{4,3},{5,4},{6,5},{7,6},{8,7},{9,8},{10,9},{11,1... | collective-permute-start | bytes 6152 | tf_op jit(solution)/shard_map/ppermute | solution.py:25
  180.1 7.1 %collective-permute-start.28 = (f32[4,1,128]{2,1,0:T(1,128)S(1)}, f32[4,1,128]{2,1,0:T(1,128)S(1)}, u32[]{:S(2)}, u32[]{:S(2)}) collective-permute-start(f32[4,1,128]{2,1,0:T(1,128)S(1)} %get-tuple-element.191), channel_id=1, source_target_pairs={{0,1},{1,2},{2,3},{3,4},{4,5},{5,6},{6,7},{7,8},{8,9},{9,10},{10,1... | collective-permute-start | bytes 6152 | tf_op jit(solution)/shard_map/ppermute | solution.py:22
  185.7 3.1 %collective-permute-start.29 = (f32[4,1,128]{2,1,0:T(1,128)S(1)}, f32[4,1,128]{2,1,0:T(1,128)S(1)}, u32[]{:S(2)}, u32[]{:S(2)}) collective-permute-start(f32[4,1,128]{2,1,0:T(1,128)S(1)} %get-tuple-element.190), channel_id=1, source_target_pairs={{1,0},{2,1},{3,2},{4,3},{5,4},{6,5},{7,6},{8,7},{9,8},{10,9},{11,1... | collective-permute-start | bytes 6152 | tf_op jit(solution)/shard_map/ppermute | solution.py:25
  189.0 7.1 %collective-permute-start.30 = (f32[4,1,128]{2,1,0:T(1,128)S(1)}, f32[4,1,128]{2,1,0:T(1,128)S(1)}, u32[]{:S(2)}, u32[]{:S(2)}) collective-permute-start(f32[4,1,128]{2,1,0:T(1,128)S(1)} %get-tuple-element.187), channel_id=1, source_target_pairs={{0,1},{1,2},{2,3},{3,4},{4,5},{5,6},{6,7},{7,8},{8,9},{9,10},{10,1... | collective-permute-start | bytes 6152 | tf_op jit(solution)/shard_map/ppermute | solution.py:22
  194.6 3.1 %collective-permute-start.31 = (f32[4,1,128]{2,1,0:T(1,128)S(1)}, f32[4,1,128]{2,1,0:T(1,128)S(1)}, u32[]{:S(2)}, u32[]{:S(2)}) collective-permute-start(f32[4,1,128]{2,1,0:T(1,128)S(1)} %get-tuple-element.186), channel_id=1, source_target_pairs={{1,0},{2,1},{3,2},{4,3},{5,4},{6,5},{7,6},{8,7},{9,8},{10,9},{11,1... | collective-permute-start | bytes 6152 | tf_op jit(solution)/shard_map/ppermute | solution.py:25
  197.8 7.1 %collective-permute-start.32 = (f32[4,1,128]{2,1,0:T(1,128)S(1)}, f32[4,1,128]{2,1,0:T(1,128)S(1)}, u32[]{:S(2)}, u32[]{:S(2)}) collective-permute-start(f32[4,1,128]{2,1,0:T(1,128)S(1)} %get-tuple-element.183), channel_id=1, source_target_pairs={{0,1},{1,2},{2,3},{3,4},{4,5},{5,6},{6,7},{7,8},{8,9},{9,10},{10,1... | collective-permute-start | bytes 6152 | tf_op jit(solution)/shard_map/ppermute | solution.py:22
  203.4 3.1 %collective-permute-start.33 = (f32[4,1,128]{2,1,0:T(1,128)S(1)}, f32[4,1,128]{2,1,0:T(1,128)S(1)}, u32[]{:S(2)}, u32[]{:S(2)}) collective-permute-start(f32[4,1,128]{2,1,0:T(1,128)S(1)} %get-tuple-element.182), channel_id=1, source_target_pairs={{1,0},{2,1},{3,2},{4,3},{5,4},{6,5},{7,6},{8,7},{9,8},{10,9},{11,1... | collective-permute-start | bytes 6152 | tf_op jit(solution)/shard_map/ppermute | solution.py:25
  250.9 0.7 copy-start.8
Sparse Core Ops, SparseCore 0:
  11.4 36.8 reduce-scatter.2
  50.6 19.0 reduce-scatter.4
where the time goes:
time: 260 us; the launch traced here: 258 us
  starting transfers between devices  107 us (41%)
  waiting for transfers between devices  76.9 us (30%)
  blocking collectives  41.7 us (16%)
  between operations  15.3 us (6%)
  local copies, waits for them, and re-layouts  9.51 us (4%)
  other arithmetic  6.66 us (3%)
    ppermute x18, starting transfers between devices, with_halo(): lax.ppermute(lax.slice_in_dim(block, block.shape[dim] - width, None, axis...  83.5 us
    all_gather x1, blocking collectives, shards(): shard_rows = lax.all_gather(surface, ('comp', 'dom'), axis=1, tiled=True)  41.7 us
    reduce_scatter x1, waiting for transfers between devices, shards(): lax.psum_scatter(dense_terms, 'dom', scatter_dimension=0, tiled=True)  31.5 us
    ppermute x18, waiting for transfers between devices, with_halo(): lax.ppermute(lax.slice_in_dim(block, 0, width, axis=dim), axis, backward)  25.4 us
    ppermute x18, starting transfers between devices, with_halo(): lax.ppermute(lax.slice_in_dim(block, 0, width, axis=dim), axis, backward)  23.3 us
    reduce_scatter x1, waiting for transfers between devices, shards(): lax.psum_scatter(block_sums, 'comp', scatter_dimension=0, tiled=True)  20 us
  transfers between devices with their start and end apart: 38, of which 17 were waited for; matrix products, arithmetic and copies ran while one was open for 3% of the time, Pallas kernels for 0%

commit v1 on v0

v1 whole, which is shorter than its diff:
```python
import functools

import jax
import jax.numpy as jnp
from jax import lax
from jax.experimental import pallas as pl
from jax.experimental.pallas import tpu as pltpu
from jax.sharding import PartitionSpec as P

NSTEP = 2
NSUB = 8

wave_gain = 0.35
stress_gain = 0.1
fresh_gain = 0.1
spread_gain = 0.2
heating_gain = 0.5

MESH = pl.DeviceIdType.MESH
F32 = jnp.float32
BF16 = jnp.bfloat16


def idiv(value, by):
    if by & (by - 1) == 0:
        return lax.shift_right_logical(value, jnp.full_like(value, by.bit_length() - 1))
    return value // by


def imod(value, by):
    if by & (by - 1) == 0:
        return value & (by - 1)
    return value % by


def wrapped(value, count):
    value = jnp.where(value >= count, value - count, value)
    return jnp.where(value < 0, value + count, value)


def iota(shape, dim):
    return lax.broadcasted_iota(jnp.int32, shape, dim)


def east(v):
    return pltpu.roll(v, v.shape[-1] - 1, v.ndim - 1)


def west(v):
    return pltpu.roll(v, 1, v.ndim - 1)


def north(v):
    return pltpu.roll(v, v.shape[-2] - 1, v.ndim - 2)


def south(v):
    return pltpu.roll(v, 1, v.ndim - 2)


def kernel(
    count,
    blocks_dom,
    air_ref,
    weight_ref,
    target_ref,
    tracer_ref,
    mix_ref,
    height_ref,
    flow_ref,
    wet_ref,
    out_tracer,
    out_height,
    out_air,
    terms,
    dense,
    flux_in,
    base_out,
    base_in,
    edge_out,
    edge_in,
    force_out,
    force_in,
    second_out,
    second_in,
    surface_all,
    inverse,
    carry,
    ratio,
    response,
    work,
    flux_sems,
    base_send,
    base_recv,
    edge_send,
    edge_recv,
    force_send,
    force_recv,
    second_send,
    second_recv,
    surface_sems,
):
    group, block = lax.axis_index("comp"), lax.axis_index("dom")
    me = group * blocks_dom + block
    fields = air_ref.shape[1]
    sources, links, cols, width = weight_ref.shape[1:]
    levels, rows = tracer_ref.shape[:2]
    steps = NSTEP * NSUB
    reach = -(-steps // rows)
    offsets = [d for d in range(-reach, reach + 1) if d != 0]
    pair = 2 if sources % 2 == 0 else 1

    def device(offset):
        peer = lax.rem(me + offset + count, count)
        return (peer // blocks_dom, lax.rem(peer, blocks_dom))

    def copy_to(offset, src, dst, send, recv):
        return pltpu.make_async_remote_copy(
            src_ref=src,
            dst_ref=dst,
            send_sem=send,
            recv_sem=recv,
            device_id=device(offset),
            device_id_type=MESH,
        )

    barrier = pltpu.get_barrier_semaphore()

    def greet(offset, _):
        pl.semaphore_signal(barrier, inc=1, device_id=device(offset), device_id_type=MESH)
        return 0

    lax.fori_loop(1, count, greet, 0)

    wet = wet_ref[...].astype(F32)
    base_out[pl.ds(0, rows), :] = height_ref[...]
    base_out[pl.ds(rows, rows), :] = flow_ref[0]
    base_out[pl.ds(2 * rows, rows), :] = flow_ref[1]
    base_out[pl.ds(3 * rows, rows), :] = wet
    edge_out[0, pl.ds(0, levels), :] = tracer_ref[:, rows - 1, :]
    edge_out[1, pl.ds(0, levels), :] = tracer_ref[:, 0, :]
    edge_out[0, pl.ds(levels, rows), :] = wet
    edge_out[1, pl.ds(levels, rows), :] = wet

    exchange = air_ref[0].astype(F32)
    group_rows = pair * fields
    own = idiv(iota((group_rows, pair * cols), 0), fields) == idiv(
        iota((group_rows, pair * cols), 1), cols
    )
    for p in range(sources // pair):
        part = exchange[:, p * pair * cols : (p + 1) * pair * cols]
        lhs = jnp.where(own, jnp.concatenate([part] * pair, axis=0), 0.0).astype(BF16)
        for k in range(links):
            rhs = weight_ref[0, pl.ds(p * pair, pair), k].reshape(pair * cols, width)
            terms[pl.ds((p * links + k) * group_rows, group_rows), :] = jnp.dot(
                lhs, rhs, preferred_element_type=F32
            )
    every = sources * links * fields
    target = target_ref[0]
    lane = iota((sources, every), 1)
    lane_field = imod(lane, fields)
    lane_source = idiv(lane, group_rows * links) * pair + imod(idiv(lane, fields), pair)
    lane_link = imod(idiv(lane, group_rows), links)
    here = lane_source == iota((sources, every), 0)
    lane_target = jnp.zeros((sources, every), jnp.int32)
    for k in range(links):
        lane_target = jnp.where(here & (lane_link == k), target[:, k : k + 1], lane_target)
    lane_target = jnp.sum(lane_target, axis=0, keepdims=True)
    lane_key = lane_target * fields + lane_field[:1]
    value = terms[...]
    upper = value.astype(BF16)
    lower = (value - upper.astype(F32)).astype(BF16)
    split = jnp.concatenate([upper, lower], axis=0)

    pl.semaphore_wait(barrier, count - 1)

    edges = [
        copy_to(1, edge_out.at[0], edge_in.at[0], edge_send.at[0], edge_recv.at[0]),
        copy_to(-1, edge_out.at[1], edge_in.at[1], edge_send.at[1], edge_recv.at[1]),
    ]
    for copy in edges:
        copy.start()

    chunk = 8 if count % 8 == 0 else 1
    shape = (chunk, fields, rows, every)

    def place(c, _):
        slot = iota(shape, 0) + c * chunk
        row_key = (wrapped(slot + me, count) * rows + iota(shape, 2)) * fields + iota(shape, 1)
        row_key = row_key.reshape(chunk * fields * rows, every)
        hot = jnp.where(row_key == lane_key, 1.0, 0.0).astype(BF16)
        hot = jnp.concatenate([hot, hot], axis=1)
        placed = jnp.dot(hot, split, preferred_element_type=F32)
        dense[pl.ds(c * chunk, chunk)] = placed.astype(BF16).reshape(
            chunk, fields * rows, width
        )

        def send(b, _):
            slot = c * chunk + b

            @pl.when(slot > 0)
            def _():
                copy_to(
                    slot, dense.at[slot], flux_in.at[slot], flux_sems.at[0], flux_sems.at[1]
                ).start()

            return 0

        lax.fori_loop(0, chunk, send, 0)
        return 0

    lax.fori_loop(0, count // chunk, place, 0)

    bases = []
    for i, offset in enumerate(offsets):
        arrives = offsets.index(-offset)
        bases.append(
            copy_to(offset, base_out, base_in.at[arrives], base_send.at[i], base_recv.at[arrives])
        )
    for copy in bases:
        copy.start()

    zero = jnp.zeros((rows, width), F32)
    last_ratio = None
    last_response = None
    for l in range(levels):
        up = mix_ref[l - 1] if l > 0 else zero
        down = mix_ref[l] if l < levels - 1 else zero
        pivot = 1.0 + up + down
        if l > 0:
            pivot = pivot - up * last_ratio
        inv = 1.0 / pivot
        inverse[l] = inv
        carry[l] = up * inv
        last_response = inv if l == 0 else up * inv * last_response
        response[l] = last_response
        last_ratio = down * inv
        ratio[l] = last_ratio
    for l in range(levels - 2, -1, -1):
        last_response = response[l] + ratio[l] * last_response
        response[l] = last_response

    for copy in edges:
        copy.wait_recv()
    row = iota((rows, width), 0)
    top = row == rows - 1
    bottom = row == 0
    wet_north = jnp.where(top, edge_in[1, pl.ds(levels, 1), :], north(wet))
    wet_south = jnp.where(bottom, edge_in[0, pl.ds(levels + rows - 1, 1), :], south(wet))
    inside_top = jnp.logical_not(top & (me == count - 1))
    inside_bottom = jnp.logical_not(bottom & (me == 0))
    mix_east = spread_gain * wet * east(wet)
    mix_west = spread_gain * wet * west(wet)
    mix_north = jnp.where(inside_top, spread_gain * wet * wet_north, 0.0)
    mix_south = jnp.where(inside_bottom, spread_gain * wet * wet_south, 0.0)
    mix_own = 1.0 - (mix_east + mix_west + mix_north + mix_south)

    def solve(source, halo, result, gain):
        swept = None
        for l in range(levels):
            v = source[l]
            v_north = jnp.where(top, halo[1, pl.ds(l, 1), :], north(v))
            v_south = jnp.where(bottom, halo[0, pl.ds(l, 1), :], south(v))
            explicit = (
                mix_own * v
                + mix_east * east(v)
                + mix_west * west(v)
                + mix_north * v_north
                + mix_south * v_south
            )
            if l == 0 and gain is not None:
                explicit = explicit + gain
            swept = explicit * inverse[l] if l == 0 else explicit * inverse[l] + carry[l] * swept
            result[l] = swept
        for l in range(levels - 2, -1, -1):
            swept = result[l] + ratio[l] * swept
            result[l] = swept

    solve(tracer_ref, edge_in, work, None)

    whole = copy_to(
        1,
        dense.at[pl.ds(1, count - 1)],
        flux_in.at[pl.ds(1, count - 1)],
        flux_sems.at[0],
        flux_sems.at[1],
    )
    whole.wait_recv()

    flux = lax.fori_loop(
        1, count, lambda j, total: total + flux_in[j].astype(F32), dense[0].astype(F32)
    )
    heating = flux[0:rows]
    fresh = flux[rows : 2 * rows]
    force_out[pl.ds(0, rows), :] = fresh * wet
    force_out[pl.ds(rows, 2 * rows), :] = flux[2 * rows : 4 * rows]
    forces = []
    for i, offset in enumerate(offsets):
        arrives = offsets.index(-offset)
        forces.append(
            copy_to(
                offset, force_out, force_in.at[arrives], force_send.at[i], force_recv.at[arrives]
            )
        )
    for copy in forces:
        copy.start()

    heat = heating_gain * heating * wet
    for l in range(levels):
        work[l] = work[l] + heat * response[l]
    second_out[0] = work[:, rows - 1, :]
    second_out[1] = work[:, 0, :]
    seconds = [
        copy_to(1, second_out.at[0], second_in.at[0], second_send.at[0], second_recv.at[0]),
        copy_to(-1, second_out.at[1], second_in.at[1], second_send.at[1], second_recv.at[1]),
    ]
    for copy in seconds:
        copy.start()

    for copy in bases:
        copy.wait_recv()

    def window(own_ref, arrived, start):
        parts = []
        for offset in range(-reach, reach + 1):
            if offset == 0:
                parts.append(own_ref[pl.ds(start, rows), :])
            else:
                parts.append(arrived[offsets.index(offset), pl.ds(start, rows), :])
        return jnp.concatenate(parts, axis=0)

    tall = (2 * reach + 1) * rows
    height = window(base_out, base_in, 0)
    flow_east = window(base_out, base_in, rows)
    flow_north = window(base_out, base_in, 2 * rows)
    wet_tall = window(base_out, base_in, 3 * rows)
    number = wrapped(me * rows - reach * rows + iota((tall, width), 0), count * rows)
    face_east = wet_tall * east(wet_tall)
    face_north = jnp.where(number == count * rows - 1, 0.0, wet_tall * north(wet_tall))
    face_west = west(face_east)
    face_south = south(face_north)
    square = wave_gain * wave_gain
    gain_east = square * face_east
    gain_west = square * face_west
    gain_north = square * face_north
    gain_south = square * face_south
    gain_own = gain_east + gain_west + gain_north + gain_south
    flow_east = wave_gain * face_east * flow_east
    flow_north = wave_gain * face_north * flow_north
    spread = flow_east - west(flow_east) + flow_north - south(flow_north)

    for copy in forces:
        copy.wait_recv()
    fresh_tall = fresh_gain * window(force_out, force_in, 0)
    push_east = (wave_gain * stress_gain) * face_east * window(force_out, force_in, rows)
    push_north = (wave_gain * stress_gain) * face_north * window(force_out, force_in, 2 * rows)
    push = push_east - west(push_east) + push_north - south(push_north)

    left = steps
    for stage in range(reach):
        turns = min(rows, left)
        left -= turns

        def subcycle(_, state):
            height, spread = state
            spread = (
                spread
                + push
                + gain_own * height
                - gain_east * east(height)
                - gain_west * west(height)
                - gain_north * north(height)
                - gain_south * south(height)
            )
            return height - spread + fresh_tall, spread

        height, spread = lax.fori_loop(0, turns, subcycle, (height, spread))
        trim = lambda v: v[rows:-rows]
        height, spread, push, fresh_tall = map(trim, (height, spread, push, fresh_tall))
        gain_own, gain_east, gain_west, gain_north, gain_south = map(
            trim, (gain_own, gain_east, gain_west, gain_north, gain_south)
        )
    out_height[...] = height

    for copy in seconds:
        copy.wait_recv()
    solve(work, second_in, out_tracer, heat)

    surface_all[0] = jnp.concatenate([out_tracer[0], height], axis=0).astype(BF16)

    def share(slot, _):
        copy_to(
            slot, surface_all.at[0], surface_all.at[slot], surface_sems.at[0], surface_sems.at[1]
        ).start()
        return 0

    lax.fori_loop(1, count, share, 0)

    high = 2 * rows
    spot = iota((sources, count * high), 1)
    spot_row = wrapped(me - idiv(spot, high), count) * rows + imod(spot, rows)
    spot_field = idiv(imod(spot, high), rows)
    picks = []
    for k in range(links):
        match = spot_row == target[:, k : k + 1]
        for f in range(2):
            picks.append(jnp.where(match & (spot_field == f), 1.0, 0.0))
    picks = jnp.concatenate(picks, axis=0).astype(BF16)

    everyone = copy_to(
        1,
        surface_all.at[pl.ds(1, count - 1)],
        surface_all.at[pl.ds(1, count - 1)],
        surface_sems.at[0],
        surface_sems.at[1],
    )
    everyone.wait_recv()
    chosen = jnp.dot(
        picks, surface_all[...].reshape(count * high, width), preferred_element_type=F32
    ).astype(BF16)
    both = 2 * sources
    chosen = jnp.concatenate([chosen[k * both : (k + 1) * both] for k in range(links)], axis=1)
    results = []
    for p in range(sources // pair):
        rhs = jnp.concatenate(
            [
                weight_ref[0, pl.ds(p * pair, pair), k].reshape(pair * cols, width)
                for k in range(links)
            ],
            axis=1,
        )
        full = lax.dot_general(
            chosen, rhs, (((1,), (1,)), ((), ())), preferred_element_type=F32
        ).reshape(2, sources, pair * cols)
        belongs = iota(full.shape, 1) == p * pair + idiv(iota(full.shape, 2), cols)
        results.append(jnp.sum(jnp.where(belongs, full, 0.0), axis=1))
    out_air[0] = jnp.concatenate(results, axis=1).astype(BF16)

    for copy in edges + bases + forces + seconds:
        copy.wait_send()
    whole.wait_send()
    everyone.wait_send()


def shards(count, blocks_dom, air, weights, targets, tracer, mix, height, flow, wet):
    fields = air.shape[1]
    sources, links = weights.shape[1:3]
    levels, rows, width = tracer.shape
    sides = 2 * -(-NSTEP * NSUB // rows)
    column = pltpu.VMEM((levels, rows, width), F32)
    spec = pl.BlockSpec(memory_space=pltpu.VMEM)
    dma = pltpu.SemaphoreType.DMA
    return pl.pallas_call(
        functools.partial(kernel, count, blocks_dom),
        out_shape=(
            jax.ShapeDtypeStruct(tracer.shape, F32),
            jax.ShapeDtypeStruct(height.shape, F32),
            jax.ShapeDtypeStruct((1, 2, air.shape[2]), BF16),
        ),
        in_specs=[spec] * 8,
        out_specs=(spec,) * 3,
        scratch_shapes=[
            pltpu.VMEM((sources * links * fields, width), F32),
            pltpu.VMEM((count, fields * rows, width), BF16),
            pltpu.VMEM((count, fields * rows, width), BF16),
            pltpu.VMEM((4 * rows, width), F32),
            pltpu.VMEM((sides, 4 * rows, width), F32),
            pltpu.VMEM((2, levels + rows, width), F32),
            pltpu.VMEM((2, levels + rows, width), F32),
            pltpu.VMEM((3 * rows, width), F32),
            pltpu.VMEM((sides, 3 * rows, width), F32),
            pltpu.VMEM((2, levels, width), F32),
            pltpu.VMEM((2, levels, width), F32),
            pltpu.VMEM((count, 2 * rows, width), BF16),
            column,
            column,
            column,
            column,
            column,
            dma((2,)),
            dma((sides,)),
            dma((sides,)),
            dma((2,)),
            dma((2,)),
            dma((sides,)),
            dma((sides,)),
            dma((2,)),
            dma((2,)),
            dma((2,)),
        ],
        compiler_params=pltpu.CompilerParams(
            collective_id=0, has_side_effects=True, vmem_limit_bytes=32 * 1024 * 1024
        ),
    )(air, weights, targets, tracer, mix, height, flow, wet)


def solution(mesh):
    count = mesh.shape["comp"] * mesh.shape["dom"]
    return jax.shard_map(
        functools.partial(shards, count, mesh.shape["dom"]),
        mesh=mesh,
        in_specs=(
            P("comp", None, "dom"),
            P("comp", "dom", None, None, None),
            P("comp", "dom", None),
            P(None, ("comp", "dom"), None),
            P(None, ("comp", "dom"), None),
            P(("comp", "dom"), None),
            P(None, ("comp", "dom"), None),
            P(("comp", "dom"), None),
        ),
        out_specs=(
            P(None, ("comp", "dom"), None),
            P(("comp", "dom"), None),
            P("comp", None, "dom"),
        ),
        check_vma=False,
    )
```

time: 260 us -> 34.6 us (0.13)
  starting transfers between devices: 107 us -> 0 us
  waiting for transfers between devices: 76.9 us -> 0 us
  blocking collectives: 41.7 us -> 0 us
  Pallas kernels: 0 us -> 25.9 us
  between operations: 15.3 us -> 0.65 us
  other arithmetic: 6.66 us -> 0 us
    ppermute x36 -> x0, starting transfers between devices: 107 us -> none  [the longest x18 83.5 us: with_halo(): lax.ppermute(lax.slice_in_dim(block, block.shape[dim] - width, None, axis...]
    reduce_scatter x2 -> x0, waiting for transfers between devices: 51.5 us -> none  [the longest x1 31.5 us: shards(): lax.psum_scatter(dense_terms, 'dom', scatter_dimension=0, tiled=True)]
    all_gather x1 -> x0, blocking collectives: 41.7 us -> none  [shards(): shard_rows = lax.all_gather(surface, ('comp', 'dom'), axis=1, tiled=True)]
    pallas_call x0 -> x1, Pallas kernels: none -> 25.9 us  [shards(): pl.pallas_call(functools.partial(kernel, count, blocks_dom), out_shape=(j...]
    ppermute x36 -> x0, waiting for transfers between devices: 25.4 us -> none  [the longest x18 25.4 us: with_halo(): lax.ppermute(lax.slice_in_dim(block, 0, width, axis=dim), axis, backward)]
    slice x70 -> x0, local copies, waits for them, and re-layouts: 3.04 us -> none  [the longest x16 1.19 us: shards(): jnp.roll(new_east, 1, axis=1)]
    unnamed x49 -> x18, local copies, waits for them, and re-layouts: 4.72 us -> 7.72 us
  transfers between devices with their start and end apart: 38 -> 0, of which waited for: 17 -> 0; matrix products, arithmetic and copies ran while one was open for 3% -> 0% of each run, Pallas kernels for 0% -> 0%
where the time goes in v1:
time: 34.6 us; the launch traced here: 34.3 us
  Pallas kernels  25.9 us (75%)
  local copies, waits for them, and re-layouts  7.72 us (22%)
  between operations  0.65 us (2%)
    pallas_call x1, Pallas kernels, shards(): pl.pallas_call(functools.partial(kernel, count, blocks_dom), out_shape=(j...  25.9 us
    unnamed x18, local copies, waits for them, and re-layouts  7.72 us

profile of v1, /device:TPU:0, one launch (start us, length us, event | category | flops | bytes accessed | tf_op | source)
XLA Modules:
  0.0 34.3 jit_solution(7914141117528509931)
XLA Ops:
  0.6 0.0 copy-start.5
  0.6 0.8 %copy.11.target_ref = s32[1,8,4]{2,1,0:T(8,128)S(1)} copy(s32[1,8,4]{1,2,0:T(4,128)} %param.10) | data formatting | bytes 256 | tf_op args[2]
  1.4 0.0 copy-done.5
  1.4 0.0 copy-start
  1.4 1.2 %copy-done = bf16[1,8,4,128,128]{4,3,2,1,0:T(8,128)(2,1)S(1)} copy-done((bf16[1,8,4,128,128]{4,3,2,1,0:T(8,128)(2,1)S(1)}, bf16[1,8,4,128,128]{4,3,2,1,0:T(8,128)(2,1)}, u32[]{:S(2)}) %copy-start) | copy-done | bytes 1048600
  2.6 0.0 copy-start.1
  2.6 0.9 %copy-done.1 = f32[32,8,128]{2,1,0:T(8,128)S(1)} copy-done((f32[32,8,128]{2,1,0:T(8,128)S(1)}, f32[32,8,128]{2,1,0:T(8,128)}, u32[]{:S(2)}) %copy-start.1) | copy-done | bytes 131096
  3.5 0.0 copy-start.2
  3.5 0.9 %copy-done.2 = f32[31,8,128]{2,1,0:T(8,128)S(1)} copy-done((f32[31,8,128]{2,1,0:T(8,128)S(1)}, f32[31,8,128]{2,1,0:T(8,128)}, u32[]{:S(2)}) %copy-start.2) | copy-done | bytes 127000
  4.4 0.0 copy-start.3
  4.4 0.7 %copy-done.3 = bf16[1,4,1024]{2,1,0:T(4,128)(2,1)S(1)} copy-done((bf16[1,4,1024]{2,1,0:T(4,128)(2,1)S(1)}, bf16[1,4,1024]{2,1,0:T(4,128)(2,1)}, u32[]{:S(2)}) %copy-start.3) | copy-done | bytes 8216
  5.1 0.0 copy-start.4
  5.1 0.7 %copy-done.4 = f32[2,8,128]{2,1,0:T(8,128)S(1)} copy-done((f32[2,8,128]{2,1,0:T(8,128)S(1)}, f32[2,8,128]{2,1,0:T(8,128)}, u32[]{:S(2)}) %copy-start.4) | copy-done | bytes 8216
  5.8 0.0 copy-start.6
  5.8 0.7 %copy-done.6 = s32[8,128]{1,0:T(8,128)S(1)} copy-done((s32[8,128]{1,0:T(8,128)S(1)}, s32[8,128]{1,0:T(8,128)}, u32[]{:S(2)}) %copy-start.6) | copy-done | bytes 4120
  6.5 25.9 %shard_map.103 = (f32[32,8,128]{2,1,0:T(8,128)S(1)}, f32[8,128]{1,0:T(8,128)S(1)}, bf16[1,2,1024]{2,1,0:T(2,128)(2,1)S(1)}) custom-call(bf16[1,4,1024]{2,1,0:T(4,128)(2,1)S(1)} %copy-done.3, bf16[1,8,4,128,128]{4,3,2,1,0:T(8,128)(2,1)S(1)} %copy-done, s32[1,8,4]{2,1,0:T(8,128)S(1)} %copy.11.target_ref, f32[32,8,128]{2,1,0:T(8,128)S(1)} %copy-done.1, ...), custom_call_target="tpu_custom_call" | custom-call | tf_op jit(solution)/shard_map/pallas_call | solution.py:453
  32.4 0.7 %copy.15 = f32[32,8,128]{2,1,0:T(8,128)} copy(f32[32,8,128]{2,1,0:T(8,128)S(1)} %get-tuple-element.6) | data formatting | bytes 262144
  33.1 0.6 %copy.16 = f32[8,128]{1,0:T(8,128)} copy(f32[8,128]{1,0:T(8,128)S(1)} %get-tuple-element.7) | data formatting | bytes 8192
  33.7 0.6 %copy.17 = bf16[1,2,1024]{2,1,0:T(2,128)(2,1)} copy(bf16[1,2,1024]{2,1,0:T(2,128)(2,1)S(1)} %get-tuple-element.8) | data formatting | bytes 8192
Async XLA Ops:
  0.6 0.8 %copy-start.5 = (f32[8,128]{1,0:T(8,128)S(1)}, f32[8,128]{1,0:T(8,128)}, u32[]{:S(2)}) copy-start(f32[8,128]{1,0:T(8,128)} %height_ref.1) | copy-start | bytes 12292
  1.4 1.2 %copy-start = (bf16[1,8,4,128,128]{4,3,2,1,0:T(8,128)(2,1)S(1)}, bf16[1,8,4,128,128]{4,3,2,1,0:T(8,128)(2,1)}, u32[]{:S(2)}) copy-start(bf16[1,8,4,128,128]{4,3,2,1,0:T(8,128)(2,1)} %weight_ref.1) | copy-start | bytes 3145732
  2.6 0.9 %copy-start.1 = (f32[32,8,128]{2,1,0:T(8,128)S(1)}, f32[32,8,128]{2,1,0:T(8,128)}, u32[]{:S(2)}) copy-start(f32[32,8,128]{2,1,0:T(8,128)} %tracer_ref.1) | copy-start | bytes 393220
  3.5 0.9 %copy-start.2 = (f32[31,8,128]{2,1,0:T(8,128)S(1)}, f32[31,8,128]{2,1,0:T(8,128)}, u32[]{:S(2)}) copy-start(f32[31,8,128]{2,1,0:T(8,128)} %mix_ref.1) | copy-start | bytes 380932
  4.4 0.7 %copy-start.3 = (bf16[1,4,1024]{2,1,0:T(4,128)(2,1)S(1)}, bf16[1,4,1024]{2,1,0:T(4,128)(2,1)}, u32[]{:S(2)}) copy-start(bf16[1,4,1024]{2,1,0:T(4,128)(2,1)} %air_ref.1) | copy-start | bytes 24580
  5.1 0.7 %copy-start.4 = (f32[2,8,128]{2,1,0:T(8,128)S(1)}, f32[2,8,128]{2,1,0:T(8,128)}, u32[]{:S(2)}) copy-start(f32[2,8,128]{2,1,0:T(8,128)} %flow_ref.1) | copy-start | bytes 24580
  5.8 0.7 %copy-start.6 = (s32[8,128]{1,0:T(8,128)S(1)}, s32[8,128]{1,0:T(8,128)}, u32[]{:S(2)}) copy-start(s32[8,128]{1,0:T(8,128)} %wet_ref.1) | copy-start | bytes 12292

commit v2 on v1

--- a/solution.py
+++ b/solution.py
@@ -61,17 +61,24 @@
 def kernel(
     count,
     blocks_dom,
+    air_hbm,
+    weight_hbm,
+    target_hbm,
+    tracer_hbm,
+    mix_hbm,
+    height_hbm,
+    flow_hbm,
+    wet_hbm,
+    out_tracer,
+    out_height,
+    weight_ref,
+    surface_all,
+    out_picks,
     air_ref,
-    weight_ref,
     target_ref,
     tracer_ref,
     mix_ref,
-    height_ref,
-    flow_ref,
     wet_ref,
-    out_tracer,
-    out_height,
-    out_air,
     terms,
     dense,
     flux_in,
@@ -83,12 +90,13 @@
     force_in,
     second_out,
     second_in,
-    surface_all,
     inverse,
     carry,
     ratio,
     response,
     work,
+    load_sems,
+    weight_sems,
     flux_sems,
     base_send,
     base_recv,
@@ -124,6 +132,33 @@
             device_id_type=MESH,
         )
 
+    pairs = sources // pair
+    weight_loads = [
+        pltpu.make_async_copy(
+            weight_hbm.at[:, pl.ds(p * pair, pair)],
+            weight_ref.at[:, pl.ds(p * pair, pair)],
+            weight_sems.at[p],
+        )
+        for p in range(pairs)
+    ]
+    loads = [
+        pltpu.make_async_copy(src, dst, load_sems.at[i])
+        for i, (src, dst) in enumerate(
+            [
+                (air_hbm, air_ref),
+                (target_hbm, target_ref),
+                (wet_hbm, wet_ref),
+                (tracer_hbm, tracer_ref),
+                (height_hbm, base_out.at[pl.ds(0, rows)]),
+                (flow_hbm.at[0], base_out.at[pl.ds(rows, rows)]),
+                (flow_hbm.at[1], base_out.at[pl.ds(2 * rows, rows)]),
+                (mix_hbm, mix_ref),
+            ]
+        )
+    ]
+    for copy in loads[:2] + weight_loads + loads[2:]:
+        copy.start()
+
     barrier = pltpu.get_barrier_semaphore()
 
     def greet(offset, _):
@@ -132,22 +167,15 @@
 
     lax.fori_loop(1, count, greet, 0)
 
-    wet = wet_ref[...].astype(F32)
-    base_out[pl.ds(0, rows), :] = height_ref[...]
-    base_out[pl.ds(rows, rows), :] = flow_ref[0]
-    base_out[pl.ds(2 * rows, rows), :] = flow_ref[1]
-    base_out[pl.ds(3 * rows, rows), :] = wet
-    edge_out[0, pl.ds(0, levels), :] = tracer_ref[:, rows - 1, :]
-    edge_out[1, pl.ds(0, levels), :] = tracer_ref[:, 0, :]
-    edge_out[0, pl.ds(levels, rows), :] = wet
-    edge_out[1, pl.ds(levels, rows), :] = wet
-
+    loads[0].wait()
+    loads[1].wait()
     exchange = air_ref[0].astype(F32)
     group_rows = pair * fields
     own = idiv(iota((group_rows, pair * cols), 0), fields) == idiv(
         iota((group_rows, pair * cols), 1), cols
     )
-    for p in range(sources // pair):
+    for p in range(pairs):
+        weight_loads[p].wait()
         part = exchange[:, p * pair * cols : (p + 1) * pair * cols]
         lhs = jnp.where(own, jnp.concatenate([part] * pair, axis=0), 0.0).astype(BF16)
         for k in range(links):
@@ -156,7 +184,14 @@
                 lhs, rhs, preferred_element_type=F32
             )
     every = sources * links * fields
-    target = target_ref[0]
+    diagonal = iota((sources, sources), 0) == iota((sources, sources), 1)
+    numbers = target_ref[0].astype(F32)
+    target = [
+        jnp.sum(jnp.where(diagonal, numbers[k : k + 1], 0.0), axis=1, keepdims=True).astype(
+            jnp.int32
+        )
+        for k in range(links)
+    ]
     lane = iota((sources, every), 1)
     lane_field = imod(lane, fields)
     lane_source = idiv(lane, group_rows * links) * pair + imod(idiv(lane, fields), pair)
@@ -164,13 +199,22 @@
     here = lane_source == iota((sources, every), 0)
     lane_target = jnp.zeros((sources, every), jnp.int32)
     for k in range(links):
-        lane_target = jnp.where(here & (lane_link == k), target[:, k : k + 1], lane_target)
+        lane_target = jnp.where(here & (lane_link == k), target[k], lane_target)
     lane_target = jnp.sum(lane_target, axis=0, keepdims=True)
     lane_key = lane_target * fields + lane_field[:1]
     value = terms[...]
     upper = value.astype(BF16)
     lower = (value - upper.astype(F32)).astype(BF16)
     split = jnp.concatenate([upper, lower], axis=0)
+
+    for copy in loads[2:4]:
+        copy.wait()
+    wet = wet_ref[...].astype(F32)
+    base_out[pl.ds(3 * rows, rows), :] = wet
+    edge_out[0, pl.ds(0, levels), :] = tracer_ref[:, rows - 1, :]
+    edge_out[1, pl.ds(0, levels), :] = tracer_ref[:, 0, :]
+    edge_out[0, pl.ds(levels, rows), :] = wet
+    edge_out[1, pl.ds(levels, rows), :] = wet
 
     pl.semaphore_wait(barrier, count - 1)
 
@@ -211,6 +255,8 @@
 
     lax.fori_loop(0, count // chunk, place, 0)
 
+    for copy in loads[4:]:
+        copy.wait()
     bases = []
     for i, offset in enumerate(offsets):
         arrives = offsets.index(-offset)
@@ -402,10 +448,10 @@
     spot_field = idiv(imod(spot, high), rows)
     picks = []
     for k in range(links):
-        match = spot_row == target[:, k : k + 1]
+        match = spot_row == target[k]
         for f in range(2):
             picks.append(jnp.where(match & (spot_field == f), 1.0, 0.0))
-    picks = jnp.concatenate(picks, axis=0).astype(BF16)
+    out_picks[...] = jnp.concatenate(picks, axis=0).astype(BF16)
 
     everyone = copy_to(
         1,
@@ -415,8 +461,34 @@
         surface_sems.at[1],
     )
     everyone.wait_recv()
+    for copy in edges + bases + forces + seconds:
+        copy.wait_send()
+    whole.wait_send()
+    everyone.wait_send()
+
+
+def finish(
+    tracer_ref,
+    height_ref,
+    weight_ref,
+    surface_ref,
+    picks_ref,
+    out_tracer,
+    out_height,
+    out_air,
+    returned,
+    sems,
+):
+    sources, links, cols, width = weight_ref.shape[1:]
+    pair = 2 if sources % 2 == 0 else 1
+    stores = [
+        pltpu.make_async_copy(tracer_ref, out_tracer, sems.at[0]),
+        pltpu.make_async_copy(height_ref, out_height, sems.at[1]),
+    ]
+    for copy in stores:
+        copy.start()
     chosen = jnp.dot(
-        picks, surface_all[...].reshape(count * high, width), preferred_element_type=F32
+        picks_ref[...], surface_ref[...].reshape(-1, width), preferred_element_type=F32
     ).astype(BF16)
     both = 2 * sources
     chosen = jnp.concatenate([chosen[k * both : (k + 1) * both] for k in range(links)], axis=1)
@@ -434,12 +506,11 @@
         ).reshape(2, sources, pair * cols)
         belongs = iota(full.shape, 1) == p * pair + idiv(iota(full.shape, 2), cols)
         results.append(jnp.sum(jnp.where(belongs, full, 0.0), axis=1))
-    out_air[0] = jnp.concatenate(results, axis=1).astype(BF16)
-
-    for copy in edges + bases + forces + seconds:
-        copy.wait_send()
-    whole.wait_send()
-    everyone.wait_send()
+    returned[0] = jnp.concatenate(results, axis=1).astype(BF16)
+    last = pltpu.make_async_copy(returned, out_air, sems.at[2])
+    last.start()
+    for copy in stores + [last]:
+        copy.wait()
 
 
 def shards(count, blocks_dom, air, weights, targets, tracer, mix, height, flow, wet):
@@ -450,16 +521,29 @@
     column = pltpu.VMEM((levels, rows, width), F32)
     spec = pl.BlockSpec(memory_space=pltpu.VMEM)
     dma = pltpu.SemaphoreType.DMA
-    return pl.pallas_call(
+    space = pl.BlockSpec(memory_space=pltpu.HBM)
+    out_air = jax.ShapeDtypeStruct((1, 2, air.shape[2]), BF16)
+    out_tracer = jax.ShapeDtypeStruct(tracer.shape, F32)
+    out_height = jax.ShapeDtypeStruct(height.shape, F32)
+    operands = (air, weights, jnp.swapaxes(targets, 1, 2), tracer, mix, height, flow, wet)
+    operands = [pltpu.with_memory_space_constraint(v, pltpu.HBM) for v in operands]
+    parts = pl.pallas_call(
         functools.partial(kernel, count, blocks_dom),
         out_shape=(
-            jax.ShapeDtypeStruct(tracer.shape, F32),
-            jax.ShapeDtypeStruct(height.shape, F32),
-            jax.ShapeDtypeStruct((1, 2, air.shape[2]), BF16),
+            out_tracer,
+            out_height,
+            jax.ShapeDtypeStruct(weights.shape, BF16),
+            jax.ShapeDtypeStruct((count, 2 * rows, width), BF16),
+            jax.ShapeDtypeStruct((2 * sources * links, count * 2 * rows), BF16),
         ),
-        in_specs=[spec] * 8,
-        out_specs=(spec,) * 3,
+        in_specs=[space] * 8,
+        out_specs=(spec,) * 5,
         scratch_shapes=[
+            pltpu.VMEM(air.shape, BF16),
+            pltpu.VMEM((1, links, sources), jnp.int32),
+            pltpu.VMEM(tracer.shape, F32),
+            pltpu.VMEM(mix.shape, F32),
+            pltpu.VMEM(wet.shape, jnp.int32),
             pltpu.VMEM((sources * links * fields, width), F32),
             pltpu.VMEM((count, fields * rows, width), BF16),
             pltpu.VMEM((count, fields * rows, width), BF16),
@@ -471,12 +555,13 @@
             pltpu.VMEM((sides, 3 * rows, width), F32),
             pltpu.VMEM((2, levels, width), F32),
             pltpu.VMEM((2, levels, width), F32),
-            pltpu.VMEM((count, 2 * rows, width), BF16),
             column,
             column,
             column,
             column,
             column,
+            dma((8,)),
+            dma((sources,)),
             dma((2,)),
             dma((sides,)),
             dma((sides,)),
@@ -491,7 +576,15 @@
         compiler_params=pltpu.CompilerParams(
             collective_id=0, has_side_effects=True, vmem_limit_bytes=32 * 1024 * 1024
         ),
-    )(air, weights, targets, tracer, mix, height, flow, wet)
+    )(*operands)
+    return pl.pallas_call(
+        finish,
+        out_shape=(out_tracer, out_height, out_air),
+        in_specs=[spec] * 5,
+        out_specs=(space,) * 3,
+        scratch_shapes=[pltpu.VMEM(out_air.shape, BF16), dma((3,))],
+        compiler_params=pltpu.CompilerParams(vmem_limit_bytes=32 * 1024 * 1024),
+    )(*parts)
 
 
 def solution(mesh):

time: 34.6 us -> 27.7 us (0.80)
  local copies, waits for them, and re-layouts: 7.72 us -> 0 us
  Pallas kernels: 25.9 us -> 26.8 us
    unnamed x18 -> x0, local copies, waits for them, and re-layouts: 7.72 us -> none
    pallas_call x1 -> x2, Pallas kernels: 25.9 us -> 26.8 us  [the longest x1 25.7 us: shards(): pl.pallas_call(functools.partial(kernel, count, blocks_dom), out_shape=(o...]
where the time goes in v2:
time: 27.7 us; the launch traced here: 27.4 us
  Pallas kernels  26.8 us (97%)
  between operations  0.64 us (2%)
    pallas_call x1, Pallas kernels, shards(): pl.pallas_call(functools.partial(kernel, count, blocks_dom), out_shape=(o...  25.7 us
    pallas_call x1, Pallas kernels, shards(): pl.pallas_call(finish, out_shape=(out_tracer, out_height, out_air), in_sp...  1.11 us

profile of v2, /device:TPU:0, one launch (start us, length us, event | category | flops | bytes accessed | tf_op | source)
XLA Modules:
  0.0 27.4 jit_solution(17573314968093735167)
XLA Ops:
  0.6 25.7 %shard_map.103 = (f32[32,8,128]{2,1,0:T(8,128)S(1)}, f32[8,128]{1,0:T(8,128)S(1)}, bf16[1,8,4,128,128]{4,3,2,1,0:T(8,128)(2,1)S(1)}, bf16[32,16,128]{2,1,0:T(8,128)(2,1)S(1)}, bf16[64,512]{1,0:T(8,128)(2,1)S(1)}) custom-call(bf16[1,4,1024]{2,1,0:T(4,128)(2,1)} %air_hbm.1, bf16[1,8,4,128,128]{4,3,2,1,0:T(8,128)(2,1)} %weight_hbm.1, s32[1,4,8]{2,1,0:T(4,128)} %bitcast.1, ...), custom_call_target="tpu_custom_call" | custom-call | tf_op jit(solution)/shard_map/pallas_call | solution.py:530
  26.3 1.1 %shard_map.104 = (f32[32,8,128]{2,1,0:T(8,128)}, f32[8,128]{1,0:T(8,128)}, bf16[1,2,1024]{2,1,0:T(2,128)(2,1)}) custom-call(f32[32,8,128]{2,1,0:T(8,128)S(1)} %get-tuple-element.8.tracer_ref, f32[8,128]{1,0:T(8,128)S(1)} %get-tuple-element.9.height_ref, bf16[1,8,4,128,128]{4,3,2,1,0:T(8,128)(2,1)S(1)} %get-tuple-element.10.weight_ref, ...), custom_call_target="tpu_custom_call" | custom-call | tf_op jit(solution)/shard_map/pallas_call | solution.py:580

commit v3 on v2

--- a/solution.py
+++ b/solution.py
@@ -59,7 +59,7 @@
 
 
 def kernel(
-    count,
+    groups,
     blocks_dom,
     air_hbm,
     weight_hbm,
@@ -82,6 +82,8 @@
     terms,
     dense,
     flux_in,
+    middle_out,
+    middle_in,
     base_out,
     base_in,
     edge_out,
@@ -98,6 +100,7 @@
     load_sems,
     weight_sems,
     flux_sems,
+    middle_sems,
     base_send,
     base_recv,
     edge_send,
@@ -106,10 +109,12 @@
     force_recv,
     second_send,
     second_recv,
+    column_sems,
     surface_sems,
 ):
     group, block = lax.axis_index("comp"), lax.axis_index("dom")
     me = group * blocks_dom + block
+    count = groups * blocks_dom
     fields = air_ref.shape[1]
     sources, links, cols, width = weight_ref.shape[1:]
     levels, rows = tracer_ref.shape[:2]
@@ -118,17 +123,23 @@
     offsets = [d for d in range(-reach, reach + 1) if d != 0]
     pair = 2 if sources % 2 == 0 else 1
 
-    def device(offset):
+    def beside(offset):
         peer = lax.rem(me + offset + count, count)
         return (peer // blocks_dom, lax.rem(peer, blocks_dom))
 
-    def copy_to(offset, src, dst, send, recv):
+    def in_group(offset):
+        return (group, lax.rem(block + offset, blocks_dom))
+
+    def across(offset):
+        return (lax.rem(group + offset, groups), block)
+
+    def copy_to(peer, src, dst, send, recv):
         return pltpu.make_async_remote_copy(
             src_ref=src,
             dst_ref=dst,
             send_sem=send,
             recv_sem=recv,
-            device_id=device(offset),
+            device_id=peer,
             device_id_type=MESH,
         )
 
@@ -161,11 +172,18 @@
 
     barrier = pltpu.get_barrier_semaphore()
 
-    def greet(offset, _):
-        pl.semaphore_signal(barrier, inc=1, device_id=device(offset), device_id_type=MESH)
+    def greet(peer):
+        pl.semaphore_signal(barrier, inc=1, device_id=peer, device_id_type=MESH)
+
+    def greet_group(offset, _):
+        greet(in_group(offset))
         return 0
 
-    lax.fori_loop(1, count, greet, 0)
+    lax.fori_loop(1, blocks_dom, greet_group, 0)
+    for offset in range(1, groups):
+        greet(across(offset))
+    for offset in offsets:
+        greet(beside(offset))
 
     loads[0].wait()
     loads[1].wait()
@@ -216,44 +234,45 @@
     edge_out[0, pl.ds(levels, rows), :] = wet
     edge_out[1, pl.ds(levels, rows), :] = wet
 
-    pl.semaphore_wait(barrier, count - 1)
+    pl.semaphore_wait(barrier, blocks_dom - 1 + groups - 1 + len(offsets))
 
     edges = [
-        copy_to(1, edge_out.at[0], edge_in.at[0], edge_send.at[0], edge_recv.at[0]),
-        copy_to(-1, edge_out.at[1], edge_in.at[1], edge_send.at[1], edge_recv.at[1]),
+        copy_to(beside(1), edge_out.at[0], edge_in.at[0], edge_send.at[0], edge_recv.at[0]),
+        copy_to(beside(-1), edge_out.at[1], edge_in.at[1], edge_send.at[1], edge_recv.at[1]),
     ]
     for copy in edges:
         copy.start()
 
-    chunk = 8 if count % 8 == 0 else 1
-    shape = (chunk, fields, rows, every)
+    chunk = 2 if blocks_dom % 2 == 0 else 1
+    shape = (chunk, groups, fields, rows, every)
 
     def place(c, _):
-        slot = iota(shape, 0) + c * chunk
-        row_key = (wrapped(slot + me, count) * rows + iota(shape, 2)) * fields + iota(shape, 1)
-        row_key = row_key.reshape(chunk * fields * rows, every)
+        to_block = wrapped(iota(shape, 0) + (c * chunk + block), blocks_dom)
+        to_group = wrapped(iota(shape, 1) + group, groups)
+        row_key = ((to_group * blocks_dom + to_block) * rows + iota(shape, 3)) * fields
+        row_key = (row_key + iota(shape, 2)).reshape(chunk * groups * fields * rows, every)
         hot = jnp.where(row_key == lane_key, 1.0, 0.0).astype(BF16)
         hot = jnp.concatenate([hot, hot], axis=1)
         placed = jnp.dot(hot, split, preferred_element_type=F32)
         dense[pl.ds(c * chunk, chunk)] = placed.astype(BF16).reshape(
-            chunk, fields * rows, width
-        )
-
-        def send(b, _):
+            chunk, groups, fields * rows, width
+        )
+        for b in range(chunk):
             slot = c * chunk + b
 
             @pl.when(slot > 0)
             def _():
                 copy_to(
-                    slot, dense.at[slot], flux_in.at[slot], flux_sems.at[0], flux_sems.at[1]
+                    in_group(slot),
+                    dense.at[slot],
+                    flux_in.at[slot],
+                    flux_sems.at[0],
+                    flux_sems.at[1],
                 ).start()
 
-            return 0
-
-        lax.fori_loop(0, chunk, send, 0)
         return 0
 
-    lax.fori_loop(0, count // chunk, place, 0)
+    lax.fori_loop(0, blocks_dom // chunk, place, 0)
 
     for copy in loads[4:]:
         copy.wait()
@@ -261,7 +280,7 @@
     for i, offset in enumerate(offsets):
         arrives = offsets.index(-offset)
         bases.append(
-            copy_to(offset, base_out, base_in.at[arrives], base_send.at[i], base_recv.at[arrives])
+            copy_to(beside(offset), base_out, base_in.at[arrives], base_send.at[i], base_recv.at[arrives])
         )
     for copy in bases:
         copy.start()
@@ -324,18 +343,31 @@
 
     solve(tracer_ref, edge_in, work, None)
 
+    others = pl.ds(1, blocks_dom - 1)
     whole = copy_to(
-        1,
-        dense.at[pl.ds(1, count - 1)],
-        flux_in.at[pl.ds(1, count - 1)],
-        flux_sems.at[0],
-        flux_sems.at[1],
+        in_group(1), dense.at[others], flux_in.at[others], flux_sems.at[0], flux_sems.at[1]
     )
     whole.wait_recv()
-
-    flux = lax.fori_loop(
-        1, count, lambda j, total: total + flux_in[j].astype(F32), dense[0].astype(F32)
-    )
+    middles = []
+    for j in list(range(1, groups)) + [0]:
+        flux = dense[0, j].astype(F32)
+        for o in range(1, blocks_dom):
+            flux = flux + flux_in[o, j].astype(F32)
+        if j > 0:
+            middle_out[j] = flux.astype(BF16)
+            middles.append(
+                copy_to(
+                    across(j),
+                    middle_out.at[j],
+                    middle_in.at[j],
+                    middle_sems.at[0, j],
+                    middle_sems.at[1, j],
+                )
+            )
+            middles[-1].start()
+    for j in range(1, groups):
+        middles[j - 1].wait_recv()
+        flux = flux + middle_in[j].astype(F32)
     heating = flux[0:rows]
     fresh = flux[rows : 2 * rows]
     force_out[pl.ds(0, rows), :] = fresh * wet
@@ -345,7 +377,11 @@
         arrives = offsets.index(-offset)
         forces.append(
             copy_to(
-                offset, force_out, force_in.at[arrives], force_send.at[i], force_recv.at[arrives]
+                beside(offset),
+                force_out,
+                force_in.at[arrives],
+                force_send.at[i],
+                force_recv.at[arrives],
             )
         )
     for copy in forces:
@@ -357,8 +393,8 @@
     second_out[0] = work[:, rows - 1, :]
     second_out[1] = work[:, 0, :]
     seconds = [
-        copy_to(1, second_out.at[0], second_in.at[0], second_send.at[0], second_recv.at[0]),
-        copy_to(-1, second_out.at[1], second_in.at[1], second_send.at[1], second_recv.at[1]),
+        copy_to(beside(1), second_out.at[0], second_in.at[0], second_send.at[0], second_recv.at[0]),
+        copy_to(beside(-1), second_out.at[1], second_in.at[1], second_send.at[1], second_recv.at[1]),
     ]
     for copy in seconds:
         copy.start()
@@ -432,19 +468,40 @@
         copy.wait_recv()
     solve(work, second_in, out_tracer, heat)
 
-    surface_all[0] = jnp.concatenate([out_tracer[0], height], axis=0).astype(BF16)
+    surface_all[0, 0] = jnp.concatenate([out_tracer[0], height], axis=0).astype(BF16)
+    columns = [
+        copy_to(
+            across(j),
+            surface_all.at[0, 0],
+            surface_all.at[0, j],
+            column_sems.at[0, j],
+            column_sems.at[1, j],
+        )
+        for j in range(1, groups)
+    ]
+    for copy in columns:
+        copy.start()
+
+    for copy in columns:
+        copy.wait_recv()
 
     def share(slot, _):
         copy_to(
-            slot, surface_all.at[0], surface_all.at[slot], surface_sems.at[0], surface_sems.at[1]
+            in_group(slot),
+            surface_all.at[0],
+            surface_all.at[slot],
+            surface_sems.at[0],
+            surface_sems.at[1],
         ).start()
         return 0
 
-    lax.fori_loop(1, count, share, 0)
+    lax.fori_loop(1, blocks_dom, share, 0)
 
     high = 2 * rows
     spot = iota((sources, count * high), 1)
-    spot_row = wrapped(me - idiv(spot, high), count) * rows + imod(spot, rows)
+    spot_block = wrapped(block - idiv(spot, high * groups), blocks_dom)
+    spot_group = wrapped(group - imod(idiv(spot, high), groups), groups)
+    spot_row = (spot_group * blocks_dom + spot_block) * rows + imod(spot, rows)
     spot_field = idiv(imod(spot, high), rows)
     picks = []
     for k in range(links):
@@ -454,16 +511,16 @@
     out_picks[...] = jnp.concatenate(picks, axis=0).astype(BF16)
 
     everyone = copy_to(
-        1,
-        surface_all.at[pl.ds(1, count - 1)],
-        surface_all.at[pl.ds(1, count - 1)],
+        in_group(1),
+        surface_all.at[others],
+        surface_all.at[others],
         surface_sems.at[0],
         surface_sems.at[1],
     )
-    everyone.wait_recv()
-    for copy in edges + bases + forces + seconds:
+    for copy in edges + bases + forces + seconds + middles + columns:
         copy.wait_send()
     whole.wait_send()
+    everyone.wait_recv()
     everyone.wait_send()
 
 
@@ -513,7 +570,7 @@
         copy.wait()
 
 
-def shards(count, blocks_dom, air, weights, targets, tracer, mix, height, flow, wet):
+def shards(groups, blocks_dom, air, weights, targets, tracer, mix, height, flow, wet):
     fields = air.shape[1]
     sources, links = weights.shape[1:3]
     levels, rows, width = tracer.shape
@@ -528,13 +585,13 @@
     operands = (air, weights, jnp.swapaxes(targets, 1, 2), tracer, mix, height, flow, wet)
     operands = [pltpu.with_memory_space_constraint(v, pltpu.HBM) for v in operands]
     parts = pl.pallas_call(
-        functools.partial(kernel, count, blocks_dom),
+        functools.partial(kernel, groups, blocks_dom),
         out_shape=(
             out_tracer,
             out_height,
             jax.ShapeDtypeStruct(weights.shape, BF16),
-            jax.ShapeDtypeStruct((count, 2 * rows, width), BF16),
-            jax.ShapeDtypeStruct((2 * sources * links, count * 2 * rows), BF16),
+            jax.ShapeDtypeStruct((blocks_dom, groups, 2 * rows, width), BF16),
+            jax.ShapeDtypeStruct((2 * sources * links, groups * blocks_dom * 2 * rows), BF16),
         ),
         in_specs=[space] * 8,
         out_specs=(spec,) * 5,
@@ -545,8 +602,10 @@
             pltpu.VMEM(mix.shape, F32),
             pltpu.VMEM(wet.shape, jnp.int32),
             pltpu.VMEM((sources * links * fields, width), F32),
-            pltpu.VMEM((count, fields * rows, width), BF16),
-            pltpu.VMEM((count, fields * rows, width), BF16),
+            pltpu.VMEM((blocks_dom, groups, fields * rows, width), BF16),
+            pltpu.VMEM((blocks_dom, groups, fields * rows, width), BF16),
+            pltpu.VMEM((groups, fields * rows, width), BF16),
+            pltpu.VMEM((groups, fields * rows, width), BF16),
             pltpu.VMEM((4 * rows, width), F32),
             pltpu.VMEM((sides, 4 * rows, width), F32),
             pltpu.VMEM((2, levels + rows, width), F32),
@@ -563,6 +622,7 @@
             dma((8,)),
             dma((sources,)),
             dma((2,)),
+            dma((2, groups)),
             dma((sides,)),
             dma((sides,)),
             dma((2,)),
@@ -571,6 +631,7 @@
             dma((sides,)),
             dma((2,)),
             dma((2,)),
+            dma((2, groups)),
             dma((2,)),
         ],
         compiler_params=pltpu.CompilerParams(
@@ -588,9 +649,8 @@
 
 
 def solution(mesh):
-    count = mesh.shape["comp"] * mesh.shape["dom"]
     return jax.shard_map(
-        functools.partial(shards, count, mesh.shape["dom"]),
+        functools.partial(shards, mesh.shape["comp"], mesh.shape["dom"]),
         mesh=mesh,
         in_specs=(
             P("comp", None, "dom"),

time: 27.7 us -> 29.4 us (1.061)
  Pallas kernels: 26.8 us -> 28.5 us
    pallas_call x1, Pallas kernels: 25.7 us -> 27.4 us  [shards(): pl.pallas_call(functools.partial(kernel, groups, blocks_dom), out_shape=(...]
where the time goes in v3:
time: 29.4 us; the launch traced here: 29.2 us
  Pallas kernels  28.5 us (97%)
  between operations  0.64 us (2%)
    pallas_call x1, Pallas kernels, shards(): pl.pallas_call(functools.partial(kernel, groups, blocks_dom), out_shape=(...  27.4 us
    pallas_call x1, Pallas kernels, shards(): pl.pallas_call(finish, out_shape=(out_tracer, out_height, out_air), in_sp...  1.11 us

profile of v3, /device:TPU:0, one launch (start us, length us, event | category | flops | bytes accessed | tf_op | source)
XLA Modules:
  0.0 29.2 jit_solution(12667943071902206258)
XLA Ops:
  0.6 27.4 %shard_map.103 = (f32[32,8,128]{2,1,0:T(8,128)S(1)}, f32[8,128]{1,0:T(8,128)S(1)}, bf16[1,8,4,128,128]{4,3,2,1,0:T(8,128)(2,1)S(1)}, bf16[8,4,16,128]{3,2,1,0:T(8,128)(2,1)S(1)}, bf16[64,512]{1,0:T(8,128)(2,1)S(1)}) custom-call(bf16[1,4,1024]{2,1,0:T(4,128)(2,1)} %air_hbm.1, bf16[1,8,4,128,128]{4,3,2,1,0:T(8,128)(2,1)} %weight_hbm.1, s32[1,4,8]{2,1,0:T(4,128)} %bitcast.1, ...), custom_call_target="tpu_custom_call" | custom-call | tf_op jit(solution)/shard_map/pallas_call | solution.py:587
  28.1 1.1 %shard_map.104 = (f32[32,8,128]{2,1,0:T(8,128)}, f32[8,128]{1,0:T(8,128)}, bf16[1,2,1024]{2,1,0:T(2,128)(2,1)}) custom-call(f32[32,8,128]{2,1,0:T(8,128)S(1)} %get-tuple-element.8.tracer_ref, f32[8,128]{1,0:T(8,128)S(1)} %get-tuple-element.9.height_ref, bf16[1,8,4,128,128]{4,3,2,1,0:T(8,128)(2,1)S(1)} %get-tuple-element.10.weight_ref, ...), custom_call_target="tpu_custom_call" | custom-call | tf_op jit(solution)/shard_map/pallas_call | solution.py:641

commit v4 on v2

--- a/solution.py
+++ b/solution.py
@@ -228,7 +228,10 @@
     chunk = 8 if count % 8 == 0 else 1
     shape = (chunk, fields, rows, every)
 
-    def place(c, _):
+    chunks = count // chunk
+
+    def place(turn, _):
+        c = lax.rem(turn + 1, chunks)
         slot = iota(shape, 0) + c * chunk
         row_key = (wrapped(slot + me, count) * rows + iota(shape, 2)) * fields + iota(shape, 1)
         row_key = row_key.reshape(chunk * fields * rows, every)
@@ -253,7 +256,7 @@
         lax.fori_loop(0, chunk, send, 0)
         return 0
 
-    lax.fori_loop(0, count // chunk, place, 0)
+    lax.fori_loop(0, chunks, place, 0)
 
     for copy in loads[4:]:
         copy.wait()
@@ -301,67 +304,26 @@
     mix_south = jnp.where(inside_bottom, spread_gain * wet * wet_south, 0.0)
     mix_own = 1.0 - (mix_east + mix_west + mix_north + mix_south)
 
-    def solve(source, halo, result, gain):
+    def mixed(source, halo, l):
+        v = source[l]
+        v_north = jnp.where(top, halo[1, pl.ds(l, 1), :], north(v))
+        v_south = jnp.where(bottom, halo[0, pl.ds(l, 1), :], south(v))
+        return (
+            (mix_own * v + mix_east * east(v))
+            + mix_west * west(v)
+            + (mix_north * v_north + mix_south * v_south)
+        )
+
+    def solve(explicit, result):
         swept = None
         for l in range(levels):
-            v = source[l]
-            v_north = jnp.where(top, halo[1, pl.ds(l, 1), :], north(v))
-            v_south = jnp.where(bottom, halo[0, pl.ds(l, 1), :], south(v))
-            explicit = (
-                mix_own * v
-                + mix_east * east(v)
-                + mix_west * west(v)
-                + mix_north * v_north
-                + mix_south * v_south
-            )
-            if l == 0 and gain is not None:
-                explicit = explicit + gain
-            swept = explicit * inverse[l] if l == 0 else explicit * inverse[l] + carry[l] * swept
+            swept = explicit(l) * inverse[l] if l == 0 else explicit(l) * inverse[l] + carry[l] * swept
             result[l] = swept
         for l in range(levels - 2, -1, -1):
             swept = result[l] + ratio[l] * swept
             result[l] = swept
 
-    solve(tracer_ref, edge_in, work, None)
-
-    whole = copy_to(
-        1,
-        dense.at[pl.ds(1, count - 1)],
-        flux_in.at[pl.ds(1, count - 1)],
-        flux_sems.at[0],
-        flux_sems.at[1],
-    )
-    whole.wait_recv()
-
-    flux = lax.fori_loop(
-        1, count, lambda j, total: total + flux_in[j].astype(F32), dense[0].astype(F32)
-    )
-    heating = flux[0:rows]
-    fresh = flux[rows : 2 * rows]
-    force_out[pl.ds(0, rows), :] = fresh * wet
-    force_out[pl.ds(rows, 2 * rows), :] = flux[2 * rows : 4 * rows]
-    forces = []
-    for i, offset in enumerate(offsets):
-        arrives = offsets.index(-offset)
-        forces.append(
-            copy_to(
-                offset, force_out, force_in.at[arrives], force_send.at[i], force_recv.at[arrives]
-            )
-        )
-    for copy in forces:
-        copy.start()
-
-    heat = heating_gain * heating * wet
-    for l in range(levels):
-        work[l] = work[l] + heat * response[l]
-    second_out[0] = work[:, rows - 1, :]
-    second_out[1] = work[:, 0, :]
-    seconds = [
-        copy_to(1, second_out.at[0], second_in.at[0], second_send.at[0], second_recv.at[0]),
-        copy_to(-1, second_out.at[1], second_in.at[1], second_send.at[1], second_recv.at[1]),
-    ]
-    for copy in seconds:
-        copy.start()
+    solve(lambda l: mixed(tracer_ref, edge_in, l), work)
 
     for copy in bases:
         copy.wait_recv()
@@ -395,6 +357,52 @@
     flow_north = wave_gain * face_north * flow_north
     spread = flow_east - west(flow_east) + flow_north - south(flow_north)
 
+    whole = copy_to(
+        1,
+        dense.at[pl.ds(1, count - 1)],
+        flux_in.at[pl.ds(1, count - 1)],
+        flux_sems.at[0],
+        flux_sems.at[1],
+    )
+    whole.wait_recv()
+
+    flux_in[0] = dense[0]
+    wide = 8 if count % 8 == 0 else 1
+
+    def gather(turn, total):
+        part = flux_in[pl.ds(turn * wide, wide)].astype(F32)
+        return total + jnp.sum(part, axis=0)
+
+    flux = lax.fori_loop(
+        0, count // wide, gather, jnp.zeros((fields * rows, width), F32), unroll=count <= 32
+    )
+    heating = flux[0:rows]
+    fresh = flux[rows : 2 * rows]
+    force_out[pl.ds(0, rows), :] = fresh * wet
+    force_out[pl.ds(rows, 2 * rows), :] = flux[2 * rows : 4 * rows]
+    forces = []
+    for i, offset in enumerate(offsets):
+        arrives = offsets.index(-offset)
+        forces.append(
+            copy_to(
+                offset, force_out, force_in.at[arrives], force_send.at[i], force_recv.at[arrives]
+            )
+        )
+    for copy in forces:
+        copy.start()
+
+    heat = heating_gain * heating * wet
+    for l in range(levels):
+        work[l] = work[l] + heat * response[l]
+    second_out[0] = work[:, rows - 1, :]
+    second_out[1] = work[:, 0, :]
+    seconds = [
+        copy_to(1, second_out.at[0], second_in.at[0], second_send.at[0], second_recv.at[0]),
+        copy_to(-1, second_out.at[1], second_in.at[1], second_send.at[1], second_recv.at[1]),
+    ]
+    for copy in seconds:
+        copy.start()
+
     for copy in forces:
         copy.wait_recv()
     fresh_tall = fresh_gain * window(force_out, force_in, 0)
@@ -409,30 +417,30 @@
 
         def subcycle(_, state):
             height, spread = state
-            spread = (
-                spread
-                + push
-                + gain_own * height
-                - gain_east * east(height)
-                - gain_west * west(height)
-                - gain_north * north(height)
-                - gain_south * south(height)
-            )
-            return height - spread + fresh_tall, spread
-
-        height, spread = lax.fori_loop(0, turns, subcycle, (height, spread))
+            here = (spread + push) + gain_own * height
+            sides = gain_east * east(height) + gain_west * west(height)
+            ends = gain_north * north(height) + gain_south * south(height)
+            spread = here - sides - ends
+            return (height + fresh_tall) - spread, spread
+
+        height, spread = lax.fori_loop(0, turns, subcycle, (height, spread), unroll=True)
         trim = lambda v: v[rows:-rows]
         height, spread, push, fresh_tall = map(trim, (height, spread, push, fresh_tall))
         gain_own, gain_east, gain_west, gain_north, gain_south = map(
             trim, (gain_own, gain_east, gain_west, gain_north, gain_south)
         )
-    out_height[...] = height
-
     for copy in seconds:
         copy.wait_recv()
-    solve(work, second_in, out_tracer, heat)
-
-    surface_all[0] = jnp.concatenate([out_tracer[0], height], axis=0).astype(BF16)
+    surface = [jnp.zeros((rows, width), F32)] * 4
+    for l in range(levels):
+        explicit = mixed(work, second_in, l)
+        if l == 0:
+            explicit = explicit + heat
+        out_tracer[l] = explicit
+        surface[l % 4] = surface[l % 4] + response[l] * explicit
+    surface = (surface[0] + surface[1]) + (surface[2] + surface[3])
+
+    surface_all[0] = jnp.concatenate([surface, height], axis=0).astype(BF16)
 
     def share(slot, _):
         copy_to(
@@ -441,6 +449,8 @@
         return 0
 
     lax.fori_loop(1, count, share, 0)
+    out_height[...] = height
+    solve(lambda l: out_tracer[l], out_tracer)
 
     high = 2 * rows
     spot = iota((sources, count * high), 1)

time: 27.7 us -> 27.1 us (0.978)
  Pallas kernels: 26.8 us -> 26.3 us
    pallas_call x1, Pallas kernels: 25.7 us -> 25.2 us  [shards(): pl.pallas_call(functools.partial(kernel, count, blocks_dom), out_shape=(o...]
where the time goes in v4:
time: 27.1 us; the launch traced here: 26.9 us
  Pallas kernels  26.3 us (97%)
  between operations  0.64 us (2%)
    pallas_call x1, Pallas kernels, shards(): pl.pallas_call(functools.partial(kernel, count, blocks_dom), out_shape=(o...  25.2 us
    pallas_call x1, Pallas kernels, shards(): pl.pallas_call(finish, out_shape=(out_tracer, out_height, out_air), in_sp...  1.11 us

profile of v4, /device:TPU:0, one launch (start us, length us, event | category | flops | bytes accessed | tf_op | source)
XLA Modules:
  0.0 26.9 jit_solution(9732291316861957019)
XLA Ops:
  0.6 25.2 %shard_map.103 = (f32[32,8,128]{2,1,0:T(8,128)S(1)}, f32[8,128]{1,0:T(8,128)S(1)}, bf16[1,8,4,128,128]{4,3,2,1,0:T(8,128)(2,1)S(1)}, bf16[32,16,128]{2,1,0:T(8,128)(2,1)S(1)}, bf16[64,512]{1,0:T(8,128)(2,1)S(1)}) custom-call(bf16[1,4,1024]{2,1,0:T(4,128)(2,1)} %air_hbm.1, bf16[1,8,4,128,128]{4,3,2,1,0:T(8,128)(2,1)} %weight_hbm.1, s32[1,4,8]{2,1,0:T(4,128)} %bitcast.1, ...), custom_call_target="tpu_custom_call" | custom-call | tf_op jit(solution)/shard_map/pallas_call | solution.py:540
  25.8 1.1 %shard_map.104 = (f32[32,8,128]{2,1,0:T(8,128)}, f32[8,128]{1,0:T(8,128)}, bf16[1,2,1024]{2,1,0:T(2,128)(2,1)}) custom-call(f32[32,8,128]{2,1,0:T(8,128)S(1)} %get-tuple-element.8.tracer_ref, f32[8,128]{1,0:T(8,128)S(1)} %get-tuple-element.9.height_ref, bf16[1,8,4,128,128]{4,3,2,1,0:T(8,128)(2,1)S(1)} %get-tuple-element.10.weight_ref, ...), custom_call_target="tpu_custom_call" | custom-call | tf_op jit(solution)/shard_map/pallas_call | solution.py:590

commit v5 on v4

--- a/solution.py
+++ b/solution.py
@@ -80,6 +80,8 @@
     mix_ref,
     wet_ref,
     terms,
+    swap_out,
+    swap_in,
     dense,
     flux_in,
     base_out,
@@ -97,6 +99,7 @@
     work,
     load_sems,
     weight_sems,
+    swap_sems,
     flux_sems,
     base_send,
     base_recv,
@@ -225,22 +228,42 @@
     for copy in edges:
         copy.start()
 
-    chunk = 8 if count % 8 == 0 else 1
+    chips = count // 2
+    chip, core = me // 2, lax.rem(me, 2)
+    sibling = 1 - 2 * core
+    chunk = 8 if chips % 8 == 0 else 1
+    chunks = chips // chunk
     shape = (chunk, fields, rows, every)
 
-    chunks = count // chunk
-
-    def place(turn, _):
-        c = lax.rem(turn + 1, chunks)
-        slot = iota(shape, 0) + c * chunk
-        row_key = (wrapped(slot + me, count) * rows + iota(shape, 2)) * fields + iota(shape, 1)
+    def placed(c, place):
+        to_chip = wrapped(iota(shape, 0) + (c * chunk + chip), chips)
+        row_key = ((to_chip * 2 + place) * rows + iota(shape, 2)) * fields + iota(shape, 1)
         row_key = row_key.reshape(chunk * fields * rows, every)
         hot = jnp.where(row_key == lane_key, 1.0, 0.0).astype(BF16)
         hot = jnp.concatenate([hot, hot], axis=1)
-        placed = jnp.dot(hot, split, preferred_element_type=F32)
-        dense[pl.ds(c * chunk, chunk)] = placed.astype(BF16).reshape(
-            chunk, fields * rows, width
-        )
+        result = jnp.dot(hot, split, preferred_element_type=F32)
+        return result.reshape(chunk, fields * rows, width)
+
+    def swap(c):
+        part = pl.ds(c * chunk, chunk)
+        return copy_to(
+            sibling, swap_out.at[part], swap_in.at[part], swap_sems.at[0, c], swap_sems.at[1, c]
+        )
+
+    def give(turn, _):
+        c = lax.rem(turn + 1, chunks)
+        swap_out[pl.ds(c * chunk, chunk)] = placed(c, 1 - core).astype(BF16)
+        swap(c).start()
+        return 0
+
+    lax.fori_loop(0, chunks, give, 0)
+
+    def keep(turn, _):
+        c = lax.rem(turn + 1, chunks)
+        part = pl.ds(c * chunk, chunk)
+        mine = placed(c, core)
+        swap(c).wait_recv()
+        dense[part] = (mine + swap_in[part].astype(F32)).astype(BF16)
 
         def send(b, _):
             slot = c * chunk + b
@@ -248,7 +271,11 @@
             @pl.when(slot > 0)
             def _():
                 copy_to(
-                    slot, dense.at[slot], flux_in.at[slot], flux_sems.at[0], flux_sems.at[1]
+                    2 * slot,
+                    dense.at[slot],
+                    flux_in.at[slot],
+                    flux_sems.at[0],
+                    flux_sems.at[1],
                 ).start()
 
             return 0
@@ -256,7 +283,7 @@
         lax.fori_loop(0, chunk, send, 0)
         return 0
 
-    lax.fori_loop(0, chunks, place, 0)
+    lax.fori_loop(0, chunks, keep, 0)
 
     for copy in loads[4:]:
         copy.wait()
@@ -357,24 +384,21 @@
     flow_north = wave_gain * face_north * flow_north
     spread = flow_east - west(flow_east) + flow_north - south(flow_north)
 
+    others = pl.ds(1, chips - 1)
     whole = copy_to(
-        1,
-        dense.at[pl.ds(1, count - 1)],
-        flux_in.at[pl.ds(1, count - 1)],
-        flux_sems.at[0],
-        flux_sems.at[1],
+        2, dense.at[others], flux_in.at[others], flux_sems.at[0], flux_sems.at[1]
     )
     whole.wait_recv()
 
     flux_in[0] = dense[0]
-    wide = 8 if count % 8 == 0 else 1
+    wide = 8 if chips % 8 == 0 else 1
 
     def gather(turn, total):
         part = flux_in[pl.ds(turn * wide, wide)].astype(F32)
         return total + jnp.sum(part, axis=0)
 
     flux = lax.fori_loop(
-        0, count // wide, gather, jnp.zeros((fields * rows, width), F32), unroll=count <= 32
+        0, chips // wide, gather, jnp.zeros((fields * rows, width), F32), unroll=chips <= 32
     )
     heating = flux[0:rows]
     fresh = flux[rows : 2 * rows]
@@ -474,6 +498,8 @@
     for copy in edges + bases + forces + seconds:
         copy.wait_send()
     whole.wait_send()
+    for c in range(chunks):
+        swap(c).wait_send()
     everyone.wait_send()
 
 
@@ -555,8 +581,7 @@
             pltpu.VMEM(mix.shape, F32),
             pltpu.VMEM(wet.shape, jnp.int32),
             pltpu.VMEM((sources * links * fields, width), F32),
-            pltpu.VMEM((count, fields * rows, width), BF16),
-            pltpu.VMEM((count, fields * rows, width), BF16),
+            *[pltpu.VMEM((count // 2, fields * rows, width), BF16)] * 4,
             pltpu.VMEM((4 * rows, width), F32),
             pltpu.VMEM((sides, 4 * rows, width), F32),
             pltpu.VMEM((2, levels + rows, width), F32),
@@ -572,6 +597,7 @@
             column,
             dma((8,)),
             dma((sources,)),
+            dma((2, count // 2)),
             dma((2,)),
             dma((sides,)),
             dma((sides,)),

time: 27.1 us -> 26.5 us (0.978)
  Pallas kernels: 26.3 us -> 25.7 us
    pallas_call x1, Pallas kernels: 25.2 us -> 24.6 us  [shards(): pl.pallas_call(functools.partial(kernel, count, blocks_dom), out_shape=(o...]
where the time goes in v5:
time: 26.5 us; the launch traced here: 26.3 us
  Pallas kernels  25.7 us (97%)
  between operations  0.64 us (2%)
    pallas_call x1, Pallas kernels, shards(): pl.pallas_call(functools.partial(kernel, count, blocks_dom), out_shape=(o...  24.6 us
    pallas_call x1, Pallas kernels, shards(): pl.pallas_call(finish, out_shape=(out_tracer, out_height, out_air), in_sp...  1.11 us

profile of v5, /device:TPU:0, one launch (start us, length us, event | category | flops | bytes accessed | tf_op | source)
XLA Modules:
  0.0 26.3 jit_solution(6423834962045576774)
XLA Ops:
  0.6 24.6 %shard_map.103 = (f32[32,8,128]{2,1,0:T(8,128)S(1)}, f32[8,128]{1,0:T(8,128)S(1)}, bf16[1,8,4,128,128]{4,3,2,1,0:T(8,128)(2,1)S(1)}, bf16[32,16,128]{2,1,0:T(8,128)(2,1)S(1)}, bf16[64,512]{1,0:T(8,128)(2,1)S(1)}) custom-call(bf16[1,4,1024]{2,1,0:T(4,128)(2,1)} %air_hbm.1, bf16[1,8,4,128,128]{4,3,2,1,0:T(8,128)(2,1)} %weight_hbm.1, s32[1,4,8]{2,1,0:T(4,128)} %bitcast.1, ...), custom_call_target="tpu_custom_call" | custom-call | tf_op jit(solution)/shard_map/pallas_call | solution.py:566
  25.2 1.1 %shard_map.104 = (f32[32,8,128]{2,1,0:T(8,128)}, f32[8,128]{1,0:T(8,128)}, bf16[1,2,1024]{2,1,0:T(2,128)(2,1)}) custom-call(f32[32,8,128]{2,1,0:T(8,128)S(1)} %get-tuple-element.8.tracer_ref, f32[8,128]{1,0:T(8,128)S(1)} %get-tuple-element.9.height_ref, bf16[1,8,4,128,128]{4,3,2,1,0:T(8,128)(2,1)S(1)} %get-tuple-element.10.weight_ref, ...), custom_call_target="tpu_custom_call" | custom-call | tf_op jit(solution)/shard_map/pallas_call | solution.py:616

commit v6 on v5

--- a/solution.py
+++ b/solution.py
@@ -436,6 +436,17 @@
 
     left = steps
     for stage in range(reach):
+        if stage == reach - 1:
+            for copy in seconds:
+                copy.wait_recv()
+            surface = [jnp.zeros((rows, width), F32)] * 4
+            for l in range(levels):
+                explicit = mixed(work, second_in, l)
+                if l == 0:
+                    explicit = explicit + heat
+                out_tracer[l] = explicit
+                surface[l % 4] = surface[l % 4] + response[l] * explicit
+            surface = (surface[0] + surface[1]) + (surface[2] + surface[3])
         turns = min(rows, left)
         left -= turns
 
@@ -453,26 +464,16 @@
         gain_own, gain_east, gain_west, gain_north, gain_south = map(
             trim, (gain_own, gain_east, gain_west, gain_north, gain_south)
         )
-    for copy in seconds:
-        copy.wait_recv()
-    surface = [jnp.zeros((rows, width), F32)] * 4
-    for l in range(levels):
-        explicit = mixed(work, second_in, l)
-        if l == 0:
-            explicit = explicit + heat
-        out_tracer[l] = explicit
-        surface[l % 4] = surface[l % 4] + response[l] * explicit
-    surface = (surface[0] + surface[1]) + (surface[2] + surface[3])
-
     surface_all[0] = jnp.concatenate([surface, height], axis=0).astype(BF16)
 
-    def share(slot, _):
+    def share(turn, _):
+        slot = 1 + lax.rem(turn + blocks_dom - 1, count - 1)
         copy_to(
             slot, surface_all.at[0], surface_all.at[slot], surface_sems.at[0], surface_sems.at[1]
         ).start()
         return 0
 
-    lax.fori_loop(1, count, share, 0)
+    lax.fori_loop(0, count - 1, share, 0)
     out_height[...] = height
     solve(lambda l: out_tracer[l], out_tracer)
 

time: 26.5 us -> 27.6 us (1.042)
  Pallas kernels: 25.7 us -> 26.8 us
    pallas_call x1, Pallas kernels: 24.6 us -> 25.7 us  [shards(): pl.pallas_call(functools.partial(kernel, count, blocks_dom), out_shape=(o...]
where the time goes in v6:
time: 27.6 us; the launch traced here: 27.4 us
  Pallas kernels  26.8 us (97%)
  between operations  0.64 us (2%)
    pallas_call x1, Pallas kernels, shards(): pl.pallas_call(functools.partial(kernel, count, blocks_dom), out_shape=(o...  25.7 us
    pallas_call x1, Pallas kernels, shards(): pl.pallas_call(finish, out_shape=(out_tracer, out_height, out_air), in_sp...  1.11 us

profile of v6, /device:TPU:0, one launch (start us, length us, event | category | flops | bytes accessed | tf_op | source)
XLA Modules:
  0.0 27.4 jit_solution(661918437779985162)
XLA Ops:
  0.6 25.7 %shard_map.103 = (f32[32,8,128]{2,1,0:T(8,128)S(1)}, f32[8,128]{1,0:T(8,128)S(1)}, bf16[1,8,4,128,128]{4,3,2,1,0:T(8,128)(2,1)S(1)}, bf16[32,16,128]{2,1,0:T(8,128)(2,1)S(1)}, bf16[64,512]{1,0:T(8,128)(2,1)S(1)}) custom-call(bf16[1,4,1024]{2,1,0:T(4,128)(2,1)} %air_hbm.1, bf16[1,8,4,128,128]{4,3,2,1,0:T(8,128)(2,1)} %weight_hbm.1, s32[1,4,8]{2,1,0:T(4,128)} %bitcast.1, ...), custom_call_target="tpu_custom_call" | custom-call | tf_op jit(solution)/shard_map/pallas_call | solution.py:567
  26.3 1.1 %shard_map.104 = (f32[32,8,128]{2,1,0:T(8,128)}, f32[8,128]{1,0:T(8,128)}, bf16[1,2,1024]{2,1,0:T(2,128)(2,1)}) custom-call(f32[32,8,128]{2,1,0:T(8,128)S(1)} %get-tuple-element.8.tracer_ref, f32[8,128]{1,0:T(8,128)S(1)} %get-tuple-element.9.height_ref, bf16[1,8,4,128,128]{4,3,2,1,0:T(8,128)(2,1)S(1)} %get-tuple-element.10.weight_ref, ...), custom_call_target="tpu_custom_call" | custom-call | tf_op jit(solution)/shard_map/pallas_call | solution.py:617
